TPU v7x, 512 devices: a whole 4x8x8 slice. The times are simulated.
512 devices in a mesh: depth: 32 (over z, x), tile: 16 (over y, core).
Axes of the slice: x: 4, y: 8, z: 8, core: 2. Of those that a mesh axis runs over, the one named last changes fastest.
Arguments:
- density: bfloat16 [1024, 128, 2048], P('depth', None, 'tile'), may hold values from 0.25 to 4
- heat: bfloat16 [1024, 128, 2048], P('depth', None, 'tile'), may hold values from 0.05 to 1
- emit_color: float32 [3], replicated, may hold values from 0.2 to 1.5
- albedo: float32 [3], replicated, may hold values from 0.2 to 1.2
- hot_order: int32 [16, 16], P('tile'), may hold values from 0 to 15, each once within a row
- hot_count: int32 [16], P('tile'), may hold values from 1 to 4, 40 in all
Outputs:
- image: float32 [4, 16, 16384], P(None, 'tile', 'depth')
Inputs may be any that keep to these rules, and one draw needn't show every extreme that they name: `hot_order`: each row lists each of the 16 bricks of its tile group once.
All inputs are finite; a program needn't handle non-finite values. No bound on the sum of `hot_count` on one device may be relied on, other than what follows from the above.
Results may differ from a plain program's by a relative error of at most 0.0033.
Values may be sent and summed in bfloat16 or wider, within the bound.
A program may use at most 64 MiB of HBM per device.

v0:
```python
import math

import jax
import jax.numpy as jnp
from jax import lax
from jax.sharding import PartitionSpec as P

BW = 32
HOT = 4


def shifted(array, axis, by):
    devices = lax.axis_size(axis)
    pairs = [(i, i + by) for i in range(devices) if 0 <= i + by < devices]
    return lax.ppermute(array, axis, pairs)


def glow(offsets, radius):
    turn = offsets * offsets % (2 * BW)
    phase = turn.astype(jnp.float32) * (math.pi / BW) + math.pi / 8.0
    ratio = offsets.astype(jnp.float32) / radius
    return jnp.cos(phase) / (1.0 + ratio * ratio)


def shards(density, heat, emit_color, albedo, hot_order, hot_count):
    depth_count = lax.axis_size("depth")
    tile_count = lax.axis_size("tile")
    slices, height, breadth = density.shape
    optical = density.astype(jnp.float32) * (1.5 / (slices * depth_count))
    slab_sum = jnp.sum(optical, axis=0)

    def pass_on(turn_index, carried):
        return shifted((carried + slab_sum).astype(jnp.bfloat16), "depth", -1).astype(jnp.float32)

    downstream = lax.fori_loop(0, depth_count - 1, pass_on, jnp.zeros_like(slab_sum))
    behind = downstream[None] + jnp.cumsum(optical[::-1], axis=0)[::-1] - optical
    lighting = jnp.exp(-behind)
    across = height // BW
    tile_index = lax.axis_index("tile")
    chosen = hot_order[0, :HOT]
    local_x = chosen % across * BW
    corner_y = chosen // across * BW
    global_x = tile_index * height + local_x
    live_mark = (jnp.arange(HOT, dtype=jnp.int32) < hot_count[0]).astype(jnp.int32)

    def cut_brick(start_y, start_x):
        return lax.dynamic_slice(heat, (jnp.int32(0), start_y, start_x), (slices, BW, BW))

    bricks = jax.vmap(cut_brick)(corner_y, local_x)
    bricks = jnp.transpose(bricks, (1, 2, 0, 3)).reshape(slices, BW, HOT * BW)
    layout_info = jnp.stack([global_x, corner_y, live_mark]).reshape(1, 3, HOT)
    scale = 64.0 / (HOT * tile_count * BW)
    inner = jnp.arange(BW, dtype=jnp.int32)
    pixels = jnp.arange(height, dtype=jnp.int32)
    screen_x = tile_index * height + pixels
    half_width = tile_count * height / 2.0
    initial = jnp.zeros((slices, height, breadth), jnp.float32)
    blocks = lax.all_gather(bricks, "tile", axis=2, tiled=True)
    layout = lax.all_gather(layout_info, "tile", axis=2, tiled=True)
    groups = layout.shape[2] // HOT

    def add_group(group_index, running):
        lead = group_index * HOT
        info = lax.dynamic_slice_in_dim(layout[0], lead, HOT, 1)
        layer = lax.dynamic_slice_in_dim(blocks, lead * BW, HOT * BW, 2).reshape(
            slices, BW, HOT, BW
        )
        offsets_x = screen_x[None, None, :] - (info[0][:, None, None] + inner[None, :, None])
        table_x = (
            scale * info[2].astype(jnp.float32)[:, None, None] * glow(offsets_x, half_width)
        ).astype(jnp.bfloat16)
        offsets_y = pixels[:, None, None] - (info[1][None, :, None] + inner[None, None, :])
        table_y = glow(offsets_y, height / 4.0).astype(jnp.bfloat16)
        spread = jnp.einsum(
            "zvhx,hxX->zhvX", layer, table_x, preferred_element_type=jnp.float32
        ).astype(jnp.bfloat16)
        return running + jnp.einsum(
            "Yhv,zhvX->zYX", table_y, spread, preferred_element_type=jnp.float32
        )

    inscatter = lax.fori_loop(0, groups, add_group, initial)
    heat_value = heat.astype(jnp.float32)
    opacity = 1.0 - jnp.exp(-optical)
    ahead = jnp.cumsum(optical, axis=0) - optical
    weight = opacity * jnp.exp(-ahead)
    lit = lighting + inscatter
    planes = []
    for channel in range(3):
        planes.append(
            jnp.sum(weight * (emit_color[channel] * heat_value + albedo[channel] * lit), axis=0)
        )
    planes.append(jnp.exp(-slab_sum))
    partial_value = jnp.stack(planes).reshape(4, depth_count, height * breadth // depth_count)
    received = lax.all_to_all(partial_value, "depth", split_axis=1, concat_axis=1, tiled=True)
    running = jnp.cumprod(received[3], axis=0)
    before = jnp.concatenate([jnp.ones_like(running[:1]), running[:-1]], axis=0)
    colors = jnp.sum(received[:3] * before[None], axis=1, keepdims=True)
    alpha = 1.0 - running[-1:][None]
    return jnp.concatenate([colors, alpha], axis=0)


def solution(mesh):
    placed = (
        P("depth", None, "tile"),
        P("depth", None, "tile"),
        P(),
        P(),
        P("tile", None),
        P("tile"),
    )
    return jax.shard_map(
        shards, mesh=mesh, in_specs=placed, out_specs=P(None, "tile", "depth"), check_vma=False
    )
```

profile of v0, /device:TPU:8, one launch (start us, length us, event | category | flops | bytes accessed | tf_op | source)
XLA Modules:
  0.0 452.3 jit_solution(16783141410948033194)
XLA Ops:
  7.3 12.5 %while.29 = (s32[]{:T(128)}, bf16[32,128,128]{2,1,0:T(8,128)(2,1)}, s32[4,3]{1,0:T(4,128)S(1)}, bf16[4,32,32,32]{3,2,1,0:T(8,128)(2,1)S(1)}, s32[]{:T(128)}) while((s32[]{:T(128)}, bf16[32,128,128]{2,1,0:T(8,128)(2,1)}, s32[4,3]{1,0:T(4,128)S(1)}, bf16[4,32,32,32]{3,2,1,0:T(8,128)(2,1)S(1)}, s32[]{:T(128)}) %tuple.90), condition=%wide.while_cond, body=%wide.while_body.sunk | while | flops 2 | bytes 327797 | solution.py:47
  22.8 20.0 %all-gather.1 = s32[16,4,3]{2,1,0:T(4,128)S(1)} all-gather(s32[1,4,3]{2,1,0:T(4,128)S(1)} %bitcast.100), channel_id=2, replica_groups=mesh['depth'=32,'tile'=16] {'tile'}, dimensions={0}, use_global_device_ids=true | all-gather | bytes 816 | tf_op jit(solution)/shard_map/all_gather | solution.py:59
  49.6 28.4 %all-gather.4.cloned.1.call-done = bf16[32,32,2048]{2,1,0:T(8,128)(2,1)} async-done(((bf16[32,32,128]{2,1,0:T(8,128)(2,1)}), bf16[32,32,2048]{2,1,0:T(8,128)(2,1)}) %all-gather.4.cloned.1.call-update) | async-done | bytes 4194320 | tf_op jit(solution)/shard_map/all_gather | solution.py:58
  78.0 53.3 %while.31 = (s32[]{:T(128)}, f32[32,128,128]{1,2,0:T(8,128)S(1)}, s32[1,3,64]{2,1,0:T(4,128)S(1)}, bf16[32,32,2048]{2,1,0:T(8,128)(2,1)}, s32[]{:T(128)}, /*inde...) while((s32[]{:T(128)}, f32[32,128,128]{1,2,0:T(8,128)S(1)}, ...), condition=%wide.region_6.7_spmd.clone.clone, body=%wide.region_5.6_spmd.clone.clone.sunk | while | flops 170082704 | bytes 5508559 | solution.py:81
  133.2 238.2 %while.30 = (s32[]{:T(128)}, f32[128,128]{1,0:T(8,128)S(1)}, f32[128,128]{1,0:T(8,128)S(1)}, s32[]{:T(128)}, s32[]{:T(128)}) while((s32[]{:T(128)}, f32[128,128]{1,0:T(8,128)S(1)}, f32[128,128]{1,0:T(8,128)S(1)}, s32[]{:T(128)}, s32[]{:T(128)}) %tuple.96), condition=%wide.region_3.0_spmd.clone, body=%wide.region_2.0_spmd.clone.sunk | while | flops 65539 | bytes 393327 | solution.py:35
  157.9 6.6 %collective-permute-done = bf16[128,128]{1,0:T(8,128)(2,1)S(1)} collective-permute-done((bf16[128,128]{1,0:T(8,128)(2,1)S(1)}, bf16[128,128]{1,0:T(8,128)(2,1)S(1)}, u32[]{:S(2)}, u32[]{:S(2)}) %collective-permute-start) | collective-permute-done | bytes 32800 | tf_op jit(solution)/shard_map/while/body/eval_jaxpr/ppermute | solution.py:15
  165.8 6.6 %collective-permute-done = bf16[128,128]{1,0:T(8,128)(2,1)S(1)} collective-permute-done((bf16[128,128]{1,0:T(8,128)(2,1)S(1)}, bf16[128,128]{1,0:T(8,128)(2,1)S(1)}, u32[]{:S(2)}, u32[]{:S(2)}) %collective-permute-start) | collective-permute-done | bytes 32800 | tf_op jit(solution)/shard_map/while/body/eval_jaxpr/ppermute | solution.py:15
  173.8 7.0 %collective-permute-done = bf16[128,128]{1,0:T(8,128)(2,1)S(1)} collective-permute-done((bf16[128,128]{1,0:T(8,128)(2,1)S(1)}, bf16[128,128]{1,0:T(8,128)(2,1)S(1)}, u32[]{:S(2)}, u32[]{:S(2)}) %collective-permute-start) | collective-permute-done | bytes 32800 | tf_op jit(solution)/shard_map/while/body/eval_jaxpr/ppermute | solution.py:15
  182.1 6.4 %collective-permute-done = bf16[128,128]{1,0:T(8,128)(2,1)S(1)} collective-permute-done((bf16[128,128]{1,0:T(8,128)(2,1)S(1)}, bf16[128,128]{1,0:T(8,128)(2,1)S(1)}, u32[]{:S(2)}, u32[]{:S(2)}) %collective-permute-start) | collective-permute-done | bytes 32800 | tf_op jit(solution)/shard_map/while/body/eval_jaxpr/ppermute | solution.py:15
  189.7 6.6 %collective-permute-done = bf16[128,128]{1,0:T(8,128)(2,1)S(1)} collective-permute-done((bf16[128,128]{1,0:T(8,128)(2,1)S(1)}, bf16[128,128]{1,0:T(8,128)(2,1)S(1)}, u32[]{:S(2)}, u32[]{:S(2)}) %collective-permute-start) | collective-permute-done | bytes 32800 | tf_op jit(solution)/shard_map/while/body/eval_jaxpr/ppermute | solution.py:15
  197.6 6.6 %collective-permute-done = bf16[128,128]{1,0:T(8,128)(2,1)S(1)} collective-permute-done((bf16[128,128]{1,0:T(8,128)(2,1)S(1)}, bf16[128,128]{1,0:T(8,128)(2,1)S(1)}, u32[]{:S(2)}, u32[]{:S(2)}) %collective-permute-start) | collective-permute-done | bytes 32800 | tf_op jit(solution)/shard_map/while/body/eval_jaxpr/ppermute | solution.py:15
  205.6 6.6 %collective-permute-done = bf16[128,128]{1,0:T(8,128)(2,1)S(1)} collective-permute-done((bf16[128,128]{1,0:T(8,128)(2,1)S(1)}, bf16[128,128]{1,0:T(8,128)(2,1)S(1)}, u32[]{:S(2)}, u32[]{:S(2)}) %collective-permute-start) | collective-permute-done | bytes 32800 | tf_op jit(solution)/shard_map/while/body/eval_jaxpr/ppermute | solution.py:15
  213.5 6.6 %collective-permute-done = bf16[128,128]{1,0:T(8,128)(2,1)S(1)} collective-permute-done((bf16[128,128]{1,0:T(8,128)(2,1)S(1)}, bf16[128,128]{1,0:T(8,128)(2,1)S(1)}, u32[]{:S(2)}, u32[]{:S(2)}) %collective-permute-start) | collective-permute-done | bytes 32800 | tf_op jit(solution)/shard_map/while/body/eval_jaxpr/ppermute | solution.py:15
  221.5 6.9 %collective-permute-done = bf16[128,128]{1,0:T(8,128)(2,1)S(1)} collective-permute-done((bf16[128,128]{1,0:T(8,128)(2,1)S(1)}, bf16[128,128]{1,0:T(8,128)(2,1)S(1)}, u32[]{:S(2)}, u32[]{:S(2)}) %collective-permute-start) | collective-permute-done | bytes 32800 | tf_op jit(solution)/shard_map/while/body/eval_jaxpr/ppermute | solution.py:15
  237.3 6.7 %collective-permute-done = bf16[128,128]{1,0:T(8,128)(2,1)S(1)} collective-permute-done((bf16[128,128]{1,0:T(8,128)(2,1)S(1)}, bf16[128,128]{1,0:T(8,128)(2,1)S(1)}, u32[]{:S(2)}, u32[]{:S(2)}) %collective-permute-start) | collective-permute-done | bytes 32800 | tf_op jit(solution)/shard_map/while/body/eval_jaxpr/ppermute | solution.py:15
  245.4 6.6 %collective-permute-done = bf16[128,128]{1,0:T(8,128)(2,1)S(1)} collective-permute-done((bf16[128,128]{1,0:T(8,128)(2,1)S(1)}, bf16[128,128]{1,0:T(8,128)(2,1)S(1)}, u32[]{:S(2)}, u32[]{:S(2)}) %collective-permute-start) | collective-permute-done | bytes 32800 | tf_op jit(solution)/shard_map/while/body/eval_jaxpr/ppermute | solution.py:15
  253.3 6.6 %collective-permute-done = bf16[128,128]{1,0:T(8,128)(2,1)S(1)} collective-permute-done((bf16[128,128]{1,0:T(8,128)(2,1)S(1)}, bf16[128,128]{1,0:T(8,128)(2,1)S(1)}, u32[]{:S(2)}, u32[]{:S(2)}) %collective-permute-start) | collective-permute-done | bytes 32800 | tf_op jit(solution)/shard_map/while/body/eval_jaxpr/ppermute | solution.py:15
  261.3 6.6 %collective-permute-done = bf16[128,128]{1,0:T(8,128)(2,1)S(1)} collective-permute-done((bf16[128,128]{1,0:T(8,128)(2,1)S(1)}, bf16[128,128]{1,0:T(8,128)(2,1)S(1)}, u32[]{:S(2)}, u32[]{:S(2)}) %collective-permute-start) | collective-permute-done | bytes 32800 | tf_op jit(solution)/shard_map/while/body/eval_jaxpr/ppermute | solution.py:15
  269.2 6.8 %collective-permute-done = bf16[128,128]{1,0:T(8,128)(2,1)S(1)} collective-permute-done((bf16[128,128]{1,0:T(8,128)(2,1)S(1)}, bf16[128,128]{1,0:T(8,128)(2,1)S(1)}, u32[]{:S(2)}, u32[]{:S(2)}) %collective-permute-start) | collective-permute-done | bytes 32800 | tf_op jit(solution)/shard_map/while/body/eval_jaxpr/ppermute | solution.py:15
  277.4 6.4 %collective-permute-done = bf16[128,128]{1,0:T(8,128)(2,1)S(1)} collective-permute-done((bf16[128,128]{1,0:T(8,128)(2,1)S(1)}, bf16[128,128]{1,0:T(8,128)(2,1)S(1)}, u32[]{:S(2)}, u32[]{:S(2)}) %collective-permute-start) | collective-permute-done | bytes 32800 | tf_op jit(solution)/shard_map/while/body/eval_jaxpr/ppermute | solution.py:15
  285.1 6.8 %collective-permute-done = bf16[128,128]{1,0:T(8,128)(2,1)S(1)} collective-permute-done((bf16[128,128]{1,0:T(8,128)(2,1)S(1)}, bf16[128,128]{1,0:T(8,128)(2,1)S(1)}, u32[]{:S(2)}, u32[]{:S(2)}) %collective-permute-start) | collective-permute-done | bytes 32800 | tf_op jit(solution)/shard_map/while/body/eval_jaxpr/ppermute | solution.py:15
  293.2 6.6 %collective-permute-done = bf16[128,128]{1,0:T(8,128)(2,1)S(1)} collective-permute-done((bf16[128,128]{1,0:T(8,128)(2,1)S(1)}, bf16[128,128]{1,0:T(8,128)(2,1)S(1)}, u32[]{:S(2)}, u32[]{:S(2)}) %collective-permute-start) | collective-permute-done | bytes 32800 | tf_op jit(solution)/shard_map/while/body/eval_jaxpr/ppermute | solution.py:15
  301.1 6.6 %collective-permute-done = bf16[128,128]{1,0:T(8,128)(2,1)S(1)} collective-permute-done((bf16[128,128]{1,0:T(8,128)(2,1)S(1)}, bf16[128,128]{1,0:T(8,128)(2,1)S(1)}, u32[]{:S(2)}, u32[]{:S(2)}) %collective-permute-start) | collective-permute-done | bytes 32800 | tf_op jit(solution)/shard_map/while/body/eval_jaxpr/ppermute | solution.py:15
  309.1 6.6 %collective-permute-done = bf16[128,128]{1,0:T(8,128)(2,1)S(1)} collective-permute-done((bf16[128,128]{1,0:T(8,128)(2,1)S(1)}, bf16[128,128]{1,0:T(8,128)(2,1)S(1)}, u32[]{:S(2)}, u32[]{:S(2)}) %collective-permute-start) | collective-permute-done | bytes 32800 | tf_op jit(solution)/shard_map/while/body/eval_jaxpr/ppermute | solution.py:15
  317.0 6.8 %collective-permute-done = bf16[128,128]{1,0:T(8,128)(2,1)S(1)} collective-permute-done((bf16[128,128]{1,0:T(8,128)(2,1)S(1)}, bf16[128,128]{1,0:T(8,128)(2,1)S(1)}, u32[]{:S(2)}, u32[]{:S(2)}) %collective-permute-start) | collective-permute-done | bytes 32800 | tf_op jit(solution)/shard_map/while/body/eval_jaxpr/ppermute | solution.py:15
  325.2 6.4 %collective-permute-done = bf16[128,128]{1,0:T(8,128)(2,1)S(1)} collective-permute-done((bf16[128,128]{1,0:T(8,128)(2,1)S(1)}, bf16[128,128]{1,0:T(8,128)(2,1)S(1)}, u32[]{:S(2)}, u32[]{:S(2)}) %collective-permute-start) | collective-permute-done | bytes 32800 | tf_op jit(solution)/shard_map/while/body/eval_jaxpr/ppermute | solution.py:15
  332.9 6.8 %collective-permute-done = bf16[128,128]{1,0:T(8,128)(2,1)S(1)} collective-permute-done((bf16[128,128]{1,0:T(8,128)(2,1)S(1)}, bf16[128,128]{1,0:T(8,128)(2,1)S(1)}, u32[]{:S(2)}, u32[]{:S(2)}) %collective-permute-start) | collective-permute-done | bytes 32800 | tf_op jit(solution)/shard_map/while/body/eval_jaxpr/ppermute | solution.py:15
  341.0 6.6 %collective-permute-done = bf16[128,128]{1,0:T(8,128)(2,1)S(1)} collective-permute-done((bf16[128,128]{1,0:T(8,128)(2,1)S(1)}, bf16[128,128]{1,0:T(8,128)(2,1)S(1)}, u32[]{:S(2)}, u32[]{:S(2)}) %collective-permute-start) | collective-permute-done | bytes 32800 | tf_op jit(solution)/shard_map/while/body/eval_jaxpr/ppermute | solution.py:15
  348.9 6.6 %collective-permute-done = bf16[128,128]{1,0:T(8,128)(2,1)S(1)} collective-permute-done((bf16[128,128]{1,0:T(8,128)(2,1)S(1)}, bf16[128,128]{1,0:T(8,128)(2,1)S(1)}, u32[]{:S(2)}, u32[]{:S(2)}) %collective-permute-start) | collective-permute-done | bytes 32800 | tf_op jit(solution)/shard_map/while/body/eval_jaxpr/ppermute | solution.py:15
  356.9 6.6 %collective-permute-done = bf16[128,128]{1,0:T(8,128)(2,1)S(1)} collective-permute-done((bf16[128,128]{1,0:T(8,128)(2,1)S(1)}, bf16[128,128]{1,0:T(8,128)(2,1)S(1)}, u32[]{:S(2)}, u32[]{:S(2)}) %collective-permute-start) | collective-permute-done | bytes 32800 | tf_op jit(solution)/shard_map/while/body/eval_jaxpr/ppermute | solution.py:15
  364.8 6.6 %collective-permute-done = bf16[128,128]{1,0:T(8,128)(2,1)S(1)} collective-permute-done((bf16[128,128]{1,0:T(8,128)(2,1)S(1)}, bf16[128,128]{1,0:T(8,128)(2,1)S(1)}, u32[]{:S(2)}, u32[]{:S(2)}) %collective-permute-start) | collective-permute-done | bytes 32800 | tf_op jit(solution)/shard_map/while/body/eval_jaxpr/ppermute | solution.py:15
  380.1 64.4 %all_to_all.5 = f32[4,32,512]{2,0,1:T(4,128)S(1)} all-to-all(f32[4,32,512]{2,0,1:T(4,128)S(1)} %pad_maximum_fusion), channel_id=1, replica_groups=mesh['depth'=32,'tile'=16] {'depth'}, dimensions={1} | all-to-all | bytes 524288 | tf_op jit(solution)/shard_map/all_to_all | solution.py:94
  (288 shorter events, 151.2 us)
Async XLA Ops:
  6.5 71.5 %all-gather.4.cloned.1.call-start = ((), (), s32[]{:S(2)}) async-start(), calls=%async_computation.1 | async-start | bytes 4456448 | tf_op jit(solution)/shard_map/all_gather | solution.py:58
  133.3 5.8 %collective-permute-start = (bf16[128,128]{1,0:T(8,128)(2,1)S(1)}, bf16[128,128]{1,0:T(8,128)(2,1)S(1)}, u32[]{:S(2)}, u32[]{:S(2)}) collective-permute-start(bf16[128,128]{1,0:T(8,128)(2,1)S(1)} %fusion.116), channel_id=1, source_target_pairs={{16,0},{32,16},{48,32},{64,48},{80,64},{96,80},{112,96},{128,112},... | collective-permute-start | bytes 98312 | tf_op jit(solution)/shard_map/while/body/eval_jaxpr/ppermute | solution.py:15
  139.1 5.8 %collective-permute-start = (bf16[128,128]{1,0:T(8,128)(2,1)S(1)}, bf16[128,128]{1,0:T(8,128)(2,1)S(1)}, u32[]{:S(2)}, u32[]{:S(2)}) collective-permute-start(bf16[128,128]{1,0:T(8,128)(2,1)S(1)} %fusion.116), channel_id=1, source_target_pairs={{16,0},{32,16},{48,32},{64,48},{80,64},{96,80},{112,96},{128,112},... | collective-permute-start | bytes 98312 | tf_op jit(solution)/shard_map/while/body/eval_jaxpr/ppermute | solution.py:15
  144.9 5.8 %collective-permute-start = (bf16[128,128]{1,0:T(8,128)(2,1)S(1)}, bf16[128,128]{1,0:T(8,128)(2,1)S(1)}, u32[]{:S(2)}, u32[]{:S(2)}) collective-permute-start(bf16[128,128]{1,0:T(8,128)(2,1)S(1)} %fusion.116), channel_id=1, source_target_pairs={{16,0},{32,16},{48,32},{64,48},{80,64},{96,80},{112,96},{128,112},... | collective-permute-start | bytes 98312 | tf_op jit(solution)/shard_map/while/body/eval_jaxpr/ppermute | solution.py:15
  150.7 5.8 %collective-permute-start = (bf16[128,128]{1,0:T(8,128)(2,1)S(1)}, bf16[128,128]{1,0:T(8,128)(2,1)S(1)}, u32[]{:S(2)}, u32[]{:S(2)}) collective-permute-start(bf16[128,128]{1,0:T(8,128)(2,1)S(1)} %fusion.116), channel_id=1, source_target_pairs={{16,0},{32,16},{48,32},{64,48},{80,64},{96,80},{112,96},{128,112},... | collective-permute-start | bytes 98312 | tf_op jit(solution)/shard_map/while/body/eval_jaxpr/ppermute | solution.py:15
  156.6 7.9 %collective-permute-start = (bf16[128,128]{1,0:T(8,128)(2,1)S(1)}, bf16[128,128]{1,0:T(8,128)(2,1)S(1)}, u32[]{:S(2)}, u32[]{:S(2)}) collective-permute-start(bf16[128,128]{1,0:T(8,128)(2,1)S(1)} %fusion.116), channel_id=1, source_target_pairs={{16,0},{32,16},{48,32},{64,48},{80,64},{96,80},{112,96},{128,112},... | collective-permute-start | bytes 98312 | tf_op jit(solution)/shard_map/while/body/eval_jaxpr/ppermute | solution.py:15
  164.5 7.9 %collective-permute-start = (bf16[128,128]{1,0:T(8,128)(2,1)S(1)}, bf16[128,128]{1,0:T(8,128)(2,1)S(1)}, u32[]{:S(2)}, u32[]{:S(2)}) collective-permute-start(bf16[128,128]{1,0:T(8,128)(2,1)S(1)} %fusion.116), channel_id=1, source_target_pairs={{16,0},{32,16},{48,32},{64,48},{80,64},{96,80},{112,96},{128,112},... | collective-permute-start | bytes 98312 | tf_op jit(solution)/shard_map/while/body/eval_jaxpr/ppermute | solution.py:15
  172.5 8.3 %collective-permute-start = (bf16[128,128]{1,0:T(8,128)(2,1)S(1)}, bf16[128,128]{1,0:T(8,128)(2,1)S(1)}, u32[]{:S(2)}, u32[]{:S(2)}) collective-permute-start(bf16[128,128]{1,0:T(8,128)(2,1)S(1)} %fusion.116), channel_id=1, source_target_pairs={{16,0},{32,16},{48,32},{64,48},{80,64},{96,80},{112,96},{128,112},... | collective-permute-start | bytes 98312 | tf_op jit(solution)/shard_map/while/body/eval_jaxpr/ppermute | solution.py:15
  180.8 7.7 %collective-permute-start = (bf16[128,128]{1,0:T(8,128)(2,1)S(1)}, bf16[128,128]{1,0:T(8,128)(2,1)S(1)}, u32[]{:S(2)}, u32[]{:S(2)}) collective-permute-start(bf16[128,128]{1,0:T(8,128)(2,1)S(1)} %fusion.116), channel_id=1, source_target_pairs={{16,0},{32,16},{48,32},{64,48},{80,64},{96,80},{112,96},{128,112},... | collective-permute-start | bytes 98312 | tf_op jit(solution)/shard_map/while/body/eval_jaxpr/ppermute | solution.py:15
  188.4 7.9 %collective-permute-start = (bf16[128,128]{1,0:T(8,128)(2,1)S(1)}, bf16[128,128]{1,0:T(8,128)(2,1)S(1)}, u32[]{:S(2)}, u32[]{:S(2)}) collective-permute-start(bf16[128,128]{1,0:T(8,128)(2,1)S(1)} %fusion.116), channel_id=1, source_target_pairs={{16,0},{32,16},{48,32},{64,48},{80,64},{96,80},{112,96},{128,112},... | collective-permute-start | bytes 98312 | tf_op jit(solution)/shard_map/while/body/eval_jaxpr/ppermute | solution.py:15
  196.3 7.9 %collective-permute-start = (bf16[128,128]{1,0:T(8,128)(2,1)S(1)}, bf16[128,128]{1,0:T(8,128)(2,1)S(1)}, u32[]{:S(2)}, u32[]{:S(2)}) collective-permute-start(bf16[128,128]{1,0:T(8,128)(2,1)S(1)} %fusion.116), channel_id=1, source_target_pairs={{16,0},{32,16},{48,32},{64,48},{80,64},{96,80},{112,96},{128,112},... | collective-permute-start | bytes 98312 | tf_op jit(solution)/shard_map/while/body/eval_jaxpr/ppermute | solution.py:15
  204.3 7.9 %collective-permute-start = (bf16[128,128]{1,0:T(8,128)(2,1)S(1)}, bf16[128,128]{1,0:T(8,128)(2,1)S(1)}, u32[]{:S(2)}, u32[]{:S(2)}) collective-permute-start(bf16[128,128]{1,0:T(8,128)(2,1)S(1)} %fusion.116), channel_id=1, source_target_pairs={{16,0},{32,16},{48,32},{64,48},{80,64},{96,80},{112,96},{128,112},... | collective-permute-start | bytes 98312 | tf_op jit(solution)/shard_map/while/body/eval_jaxpr/ppermute | solution.py:15
  212.2 7.9 %collective-permute-start = (bf16[128,128]{1,0:T(8,128)(2,1)S(1)}, bf16[128,128]{1,0:T(8,128)(2,1)S(1)}, u32[]{:S(2)}, u32[]{:S(2)}) collective-permute-start(bf16[128,128]{1,0:T(8,128)(2,1)S(1)} %fusion.116), channel_id=1, source_target_pairs={{16,0},{32,16},{48,32},{64,48},{80,64},{96,80},{112,96},{128,112},... | collective-permute-start | bytes 98312 | tf_op jit(solution)/shard_map/while/body/eval_jaxpr/ppermute | solution.py:15
  220.2 8.2 %collective-permute-start = (bf16[128,128]{1,0:T(8,128)(2,1)S(1)}, bf16[128,128]{1,0:T(8,128)(2,1)S(1)}, u32[]{:S(2)}, u32[]{:S(2)}) collective-permute-start(bf16[128,128]{1,0:T(8,128)(2,1)S(1)} %fusion.116), channel_id=1, source_target_pairs={{16,0},{32,16},{48,32},{64,48},{80,64},{96,80},{112,96},{128,112},... | collective-permute-start | bytes 98312 | tf_op jit(solution)/shard_map/while/body/eval_jaxpr/ppermute | solution.py:15
  228.4 7.7 %collective-permute-start = (bf16[128,128]{1,0:T(8,128)(2,1)S(1)}, bf16[128,128]{1,0:T(8,128)(2,1)S(1)}, u32[]{:S(2)}, u32[]{:S(2)}) collective-permute-start(bf16[128,128]{1,0:T(8,128)(2,1)S(1)} %fusion.116), channel_id=1, source_target_pairs={{16,0},{32,16},{48,32},{64,48},{80,64},{96,80},{112,96},{128,112},... | collective-permute-start | bytes 98312 | tf_op jit(solution)/shard_map/while/body/eval_jaxpr/ppermute | solution.py:15
  236.0 8.0 %collective-permute-start = (bf16[128,128]{1,0:T(8,128)(2,1)S(1)}, bf16[128,128]{1,0:T(8,128)(2,1)S(1)}, u32[]{:S(2)}, u32[]{:S(2)}) collective-permute-start(bf16[128,128]{1,0:T(8,128)(2,1)S(1)} %fusion.116), channel_id=1, source_target_pairs={{16,0},{32,16},{48,32},{64,48},{80,64},{96,80},{112,96},{128,112},... | collective-permute-start | bytes 98312 | tf_op jit(solution)/shard_map/while/body/eval_jaxpr/ppermute | solution.py:15
  244.1 7.9 %collective-permute-start = (bf16[128,128]{1,0:T(8,128)(2,1)S(1)}, bf16[128,128]{1,0:T(8,128)(2,1)S(1)}, u32[]{:S(2)}, u32[]{:S(2)}) collective-permute-start(bf16[128,128]{1,0:T(8,128)(2,1)S(1)} %fusion.116), channel_id=1, source_target_pairs={{16,0},{32,16},{48,32},{64,48},{80,64},{96,80},{112,96},{128,112},... | collective-permute-start | bytes 98312 | tf_op jit(solution)/shard_map/while/body/eval_jaxpr/ppermute | solution.py:15
  252.0 7.9 %collective-permute-start = (bf16[128,128]{1,0:T(8,128)(2,1)S(1)}, bf16[128,128]{1,0:T(8,128)(2,1)S(1)}, u32[]{:S(2)}, u32[]{:S(2)}) collective-permute-start(bf16[128,128]{1,0:T(8,128)(2,1)S(1)} %fusion.116), channel_id=1, source_target_pairs={{16,0},{32,16},{48,32},{64,48},{80,64},{96,80},{112,96},{128,112},... | collective-permute-start | bytes 98312 | tf_op jit(solution)/shard_map/while/body/eval_jaxpr/ppermute | solution.py:15
  260.0 7.9 %collective-permute-start = (bf16[128,128]{1,0:T(8,128)(2,1)S(1)}, bf16[128,128]{1,0:T(8,128)(2,1)S(1)}, u32[]{:S(2)}, u32[]{:S(2)}) collective-permute-start(bf16[128,128]{1,0:T(8,128)(2,1)S(1)} %fusion.116), channel_id=1, source_target_pairs={{16,0},{32,16},{48,32},{64,48},{80,64},{96,80},{112,96},{128,112},... | collective-permute-start | bytes 98312 | tf_op jit(solution)/shard_map/while/body/eval_jaxpr/ppermute | solution.py:15
  267.9 8.1 %collective-permute-start = (bf16[128,128]{1,0:T(8,128)(2,1)S(1)}, bf16[128,128]{1,0:T(8,128)(2,1)S(1)}, u32[]{:S(2)}, u32[]{:S(2)}) collective-permute-start(bf16[128,128]{1,0:T(8,128)(2,1)S(1)} %fusion.116), channel_id=1, source_target_pairs={{16,0},{32,16},{48,32},{64,48},{80,64},{96,80},{112,96},{128,112},... | collective-permute-start | bytes 98312 | tf_op jit(solution)/shard_map/while/body/eval_jaxpr/ppermute | solution.py:15
  276.1 7.7 %collective-permute-start = (bf16[128,128]{1,0:T(8,128)(2,1)S(1)}, bf16[128,128]{1,0:T(8,128)(2,1)S(1)}, u32[]{:S(2)}, u32[]{:S(2)}) collective-permute-start(bf16[128,128]{1,0:T(8,128)(2,1)S(1)} %fusion.116), channel_id=1, source_target_pairs={{16,0},{32,16},{48,32},{64,48},{80,64},{96,80},{112,96},{128,112},... | collective-permute-start | bytes 98312 | tf_op jit(solution)/shard_map/while/body/eval_jaxpr/ppermute | solution.py:15
  283.8 8.1 %collective-permute-start = (bf16[128,128]{1,0:T(8,128)(2,1)S(1)}, bf16[128,128]{1,0:T(8,128)(2,1)S(1)}, u32[]{:S(2)}, u32[]{:S(2)}) collective-permute-start(bf16[128,128]{1,0:T(8,128)(2,1)S(1)} %fusion.116), channel_id=1, source_target_pairs={{16,0},{32,16},{48,32},{64,48},{80,64},{96,80},{112,96},{128,112},... | collective-permute-start | bytes 98312 | tf_op jit(solution)/shard_map/while/body/eval_jaxpr/ppermute | solution.py:15
  291.9 7.9 %collective-permute-start = (bf16[128,128]{1,0:T(8,128)(2,1)S(1)}, bf16[128,128]{1,0:T(8,128)(2,1)S(1)}, u32[]{:S(2)}, u32[]{:S(2)}) collective-permute-start(bf16[128,128]{1,0:T(8,128)(2,1)S(1)} %fusion.116), channel_id=1, source_target_pairs={{16,0},{32,16},{48,32},{64,48},{80,64},{96,80},{112,96},{128,112},... | collective-permute-start | bytes 98312 | tf_op jit(solution)/shard_map/while/body/eval_jaxpr/ppermute | solution.py:15
  299.8 7.9 %collective-permute-start = (bf16[128,128]{1,0:T(8,128)(2,1)S(1)}, bf16[128,128]{1,0:T(8,128)(2,1)S(1)}, u32[]{:S(2)}, u32[]{:S(2)}) collective-permute-start(bf16[128,128]{1,0:T(8,128)(2,1)S(1)} %fusion.116), channel_id=1, source_target_pairs={{16,0},{32,16},{48,32},{64,48},{80,64},{96,80},{112,96},{128,112},... | collective-permute-start | bytes 98312 | tf_op jit(solution)/shard_map/while/body/eval_jaxpr/ppermute | solution.py:15
  307.8 7.9 %collective-permute-start = (bf16[128,128]{1,0:T(8,128)(2,1)S(1)}, bf16[128,128]{1,0:T(8,128)(2,1)S(1)}, u32[]{:S(2)}, u32[]{:S(2)}) collective-permute-start(bf16[128,128]{1,0:T(8,128)(2,1)S(1)} %fusion.116), channel_id=1, source_target_pairs={{16,0},{32,16},{48,32},{64,48},{80,64},{96,80},{112,96},{128,112},... | collective-permute-start | bytes 98312 | tf_op jit(solution)/shard_map/while/body/eval_jaxpr/ppermute | solution.py:15
  315.7 8.1 %collective-permute-start = (bf16[128,128]{1,0:T(8,128)(2,1)S(1)}, bf16[128,128]{1,0:T(8,128)(2,1)S(1)}, u32[]{:S(2)}, u32[]{:S(2)}) collective-permute-start(bf16[128,128]{1,0:T(8,128)(2,1)S(1)} %fusion.116), channel_id=1, source_target_pairs={{16,0},{32,16},{48,32},{64,48},{80,64},{96,80},{112,96},{128,112},... | collective-permute-start | bytes 98312 | tf_op jit(solution)/shard_map/while/body/eval_jaxpr/ppermute | solution.py:15
  323.9 7.7 %collective-permute-start = (bf16[128,128]{1,0:T(8,128)(2,1)S(1)}, bf16[128,128]{1,0:T(8,128)(2,1)S(1)}, u32[]{:S(2)}, u32[]{:S(2)}) collective-permute-start(bf16[128,128]{1,0:T(8,128)(2,1)S(1)} %fusion.116), channel_id=1, source_target_pairs={{16,0},{32,16},{48,32},{64,48},{80,64},{96,80},{112,96},{128,112},... | collective-permute-start | bytes 98312 | tf_op jit(solution)/shard_map/while/body/eval_jaxpr/ppermute | solution.py:15
  331.6 8.1 %collective-permute-start = (bf16[128,128]{1,0:T(8,128)(2,1)S(1)}, bf16[128,128]{1,0:T(8,128)(2,1)S(1)}, u32[]{:S(2)}, u32[]{:S(2)}) collective-permute-start(bf16[128,128]{1,0:T(8,128)(2,1)S(1)} %fusion.116), channel_id=1, source_target_pairs={{16,0},{32,16},{48,32},{64,48},{80,64},{96,80},{112,96},{128,112},... | collective-permute-start | bytes 98312 | tf_op jit(solution)/shard_map/while/body/eval_jaxpr/ppermute | solution.py:15
  339.7 7.9 %collective-permute-start = (bf16[128,128]{1,0:T(8,128)(2,1)S(1)}, bf16[128,128]{1,0:T(8,128)(2,1)S(1)}, u32[]{:S(2)}, u32[]{:S(2)}) collective-permute-start(bf16[128,128]{1,0:T(8,128)(2,1)S(1)} %fusion.116), channel_id=1, source_target_pairs={{16,0},{32,16},{48,32},{64,48},{80,64},{96,80},{112,96},{128,112},... | collective-permute-start | bytes 98312 | tf_op jit(solution)/shard_map/while/body/eval_jaxpr/ppermute | solution.py:15
  347.6 7.9 %collective-permute-start = (bf16[128,128]{1,0:T(8,128)(2,1)S(1)}, bf16[128,128]{1,0:T(8,128)(2,1)S(1)}, u32[]{:S(2)}, u32[]{:S(2)}) collective-permute-start(bf16[128,128]{1,0:T(8,128)(2,1)S(1)} %fusion.116), channel_id=1, source_target_pairs={{16,0},{32,16},{48,32},{64,48},{80,64},{96,80},{112,96},{128,112},... | collective-permute-start | bytes 98312 | tf_op jit(solution)/shard_map/while/body/eval_jaxpr/ppermute | solution.py:15
  355.6 7.9 %collective-permute-start = (bf16[128,128]{1,0:T(8,128)(2,1)S(1)}, bf16[128,128]{1,0:T(8,128)(2,1)S(1)}, u32[]{:S(2)}, u32[]{:S(2)}) collective-permute-start(bf16[128,128]{1,0:T(8,128)(2,1)S(1)} %fusion.116), channel_id=1, source_target_pairs={{16,0},{32,16},{48,32},{64,48},{80,64},{96,80},{112,96},{128,112},... | collective-permute-start | bytes 98312 | tf_op jit(solution)/shard_map/while/body/eval_jaxpr/ppermute | solution.py:15
  363.5 7.9 %collective-permute-start = (bf16[128,128]{1,0:T(8,128)(2,1)S(1)}, bf16[128,128]{1,0:T(8,128)(2,1)S(1)}, u32[]{:S(2)}, u32[]{:S(2)}) collective-permute-start(bf16[128,128]{1,0:T(8,128)(2,1)S(1)} %fusion.116), channel_id=1, source_target_pairs={{16,0},{32,16},{48,32},{64,48},{80,64},{96,80},{112,96},{128,112},... | collective-permute-start | bytes 98312 | tf_op jit(solution)/shard_map/while/body/eval_jaxpr/ppermute | solution.py:15
  (7 other events, 322.4 us)
Sparse Core Ops, SparseCore 0:
  22.1 55.9 all-gather.3
where the time goes:
time: 454 us; the launch traced here: 452 us
  waiting for transfers between devices  226 us (50%)
  blocking collectives  84.4 us (19%)
  local copies, waits for them, and re-layouts  44.1 us (10%)
  starting transfers between devices  40.1 us (9%)
  matrix products  26.6 us (6%)
  other arithmetic  16 us (4%)
  between operations  14.2 us (3%)
    ppermute x31, waiting for transfers between devices, shifted(): return lax.ppermute(array, axis, pairs)  197 us
    all_to_all x1, blocking collectives, shards(): lax.all_to_all(partial_value, 'depth', split_axis=1, concat_axis=1, tiled...  64.4 us
    ppermute x31, starting transfers between devices, shifted(): return lax.ppermute(array, axis, pairs)  40.1 us
    all_gather x1, waiting for transfers between devices, shards(): blocks = lax.all_gather(bricks, 'tile', axis=2, tiled=True)  28.4 us
    dot_general x16, matrix products, add_group(): jnp.einsum('Yhv,zhvX->zYX', table_y, spread, preferred_element_type=jnp.f...  26.6 us
    all_gather x1, blocking collectives, shards(): layout = lax.all_gather(layout_info, 'tile', axis=2, tiled=True)  20 us
    dynamic_slice x16, local copies, waits for them, and re-layouts, add_group(): lax.dynamic_slice_in_dim(blocks, lead * BW, HOT * BW, 2)  15.5 us
    gather x12, local copies, waits for them, and re-layouts  12.4 us
  transfers between devices with their start and end apart: 32, of which 32 were waited for; matrix products, arithmetic and copies ran while one was open for 2% of the time, Pallas kernels for 0%

commit v1 on v0

v1 whole, which is shorter than its diff:
```python
import functools
import math

import jax
import jax.numpy as jnp
from jax import lax
from jax.experimental import pallas as pl
from jax.experimental.pallas import tpu as pltpu
from jax.sharding import PartitionSpec as P

BW = 32
HOT = 4
QUARTERS = 4
F32 = jnp.float32
BF16 = jnp.bfloat16
MESH = pl.DeviceIdType.MESH


def iota(shape, axis):
    return lax.broadcasted_iota(jnp.int32, shape, axis)


def render(
    depth_count, tile_count,
    density_hbm, heat_hbm, emit, albedo, order, count,
    out_ref,
    density, heat, weight, blocks, spread, tables, cosines, table_y, meta, plane,
    early_out, early_in, late_out, late_in, before, base,
    copy_sem, own_send, own_recv, right_send, right_recv, left_send, left_recv,
    pair_right_send, pair_right_recv, pair_left_send, pair_left_recv,
    meta_send, meta_recv, early_send, early_recv, late_send, late_recv,
):
    slices, height, breadth = density.shape
    chips = tile_count // 2
    slots = chips - 1
    steps = 2 * slots
    zq = slices // QUARTERS
    rows = zq * BW
    band = height // depth_count
    depth = lax.axis_index("depth")
    tile = lax.axis_index("tile")
    chip = tile // 2
    core = tile % 2
    sibling = 2 * chip + 1 - core

    def at_tile(index):
        return (depth, index)

    def remote(src, dst, send, recv, device):
        return pltpu.make_async_remote_copy(
            src_ref=src, dst_ref=dst, send_sem=send, recv_sem=recv, device_id=device, device_id_type=MESH
        )

    heat_copy = pltpu.make_async_copy(heat_hbm, heat, copy_sem.at[0])
    density_copy = pltpu.make_async_copy(density_hbm, density, copy_sem.at[1])
    heat_copy.start()
    density_copy.start()

    barrier = pltpu.get_barrier_semaphore()

    @pl.loop(1, tile_count)
    def _(k):
        pl.semaphore_signal(barrier, inc=1, device_id=at_tile(lax.rem(tile + k, tile_count)), device_id_type=MESH)

    @pl.loop(1, depth_count)
    def _(k):
        pl.semaphore_signal(barrier, inc=1, device_id=(lax.rem(depth + k, depth_count), tile), device_id_type=MESH)

    across = height // BW
    lane = iota((height, breadth), 1)
    row = iota((height, breadth), 0)
    lane8 = iota((8, breadth), 1)
    row8 = iota((8, breadth), 0)
    lead = iota((across * breadth, breadth), 0) - iota((across * breadth, breadth), 1) % BW
    slot_of = iota((across * breadth, breadth), 1) // BW
    place = jnp.zeros((across * breadth, breadth), jnp.int32)
    info = jnp.zeros((8, breadth), F32)
    for s in range(HOT):
        brick = order[0, s]
        x0 = lax.rem(brick, across) * BW
        y0 = lax.div(brick, across) * BW
        dead = 1 - jnp.minimum(jnp.maximum(count[0] - s, 0), 1)
        first = lax.div(brick, across) * breadth + x0 + dead * (2 * across * breadth)
        place = jnp.where(slot_of == s, first, place)
        column = (tile * breadth + x0 + lane8 % BW).astype(F32)
        value = jnp.where(row8 == 0, y0.astype(F32), column)
        info = jnp.where(lane8 // BW == s, value, info)
    pick = jnp.where(lead == place, 1.0, 0.0).astype(BF16)
    meta[tile] = info

    heat_copy.wait()

    def pack(q):
        pieces = [
            heat[q * zq : (q + 1) * zq, m * BW : (m + 1) * BW, :].reshape(rows, breadth) for m in range(across)
        ]
        packed = jnp.dot(jnp.concatenate(pieces, axis=1), pick, preferred_element_type=F32)
        blocks[tile, q] = packed.astype(BF16)

    pack(0)
    pack(1)
    pl.semaphore_wait(barrier, tile_count + depth_count - 2)

    def part(n, sign):
        phase, slot = n // slots, lax.rem(n, slots)
        away = slot // 2
        quarter = 2 * phase + lax.rem(slot, 2) if sign < 0 else 2 * phase + 1 - lax.rem(slot, 2)
        return away, quarter

    def send(n, sign):
        away, quarter = part(n, sign)
        source = 2 * lax.rem(chip + sign * away + chips, chips) + core
        toward = 2 * lax.rem(chip - sign + chips, chips) + core
        sends, recvs = (right_send, right_recv) if sign < 0 else (left_send, left_recv)
        ref = blocks.at[source, quarter]
        return remote(ref, ref, sends.at[n], recvs.at[n], at_tile(toward))

    def arrival(n, sign):
        away, quarter = part(n, sign)
        source = lax.rem(chip + sign * (away + 1) + chips, chips)
        return source, quarter

    def received(n, sign):
        source, quarter = arrival(n, sign)
        sends, recvs = (right_send, right_recv) if sign < 0 else (left_send, left_recv)
        ref = blocks.at[2 * source + core, quarter]
        return remote(ref, ref, sends.at[n], recvs.at[n], at_tile(sibling))

    def hand_over(n, sign, mine):
        source, quarter = arrival(n, sign)
        sends, recvs = (pair_right_send, pair_right_recv) if sign < 0 else (pair_left_send, pair_left_recv)
        ref = blocks.at[2 * source + (core if mine else 1 - core), quarter]
        return remote(ref, ref, sends.at[n], recvs.at[n], at_tile(sibling))

    def own_part(q, group):
        ref = blocks.at[group, q]
        return remote(ref, ref, own_send.at[q], own_recv.at[q], at_tile(sibling))

    def meta_part(k, group):
        ref = meta.at[group]
        return remote(ref, ref, meta_send.at[k], meta_recv.at[k], at_tile(lax.rem(tile + k, tile_count)))

    def early_part(k, target, source):
        return remote(
            early_out.at[target], early_in.at[source], early_send.at[k], early_recv.at[k], (target, tile)
        )

    def late_part(k, target, source):
        return remote(late_out.at[target], late_in.at[source], late_send.at[k], late_recv.at[k], (target, tile))

    send(0, -1).start()
    send(0, 1).start()
    send(1, -1).start()
    send(1, 1).start()

    @pl.loop(1, tile_count)
    def _(k):
        meta_part(k, tile).start()

    own_part(0, tile).start()
    own_part(1, tile).start()
    pack(2)
    pack(3)
    own_part(2, tile).start()
    own_part(3, tile).start()

    offset = iota((BW, breadth), 0) - iota((BW, breadth), 1)
    turn = (offset * offset) % (2 * BW)
    chirp = jnp.cos(turn.astype(F32) * (math.pi / BW) + math.pi / 8.0)
    for s in range(height // BW):
        cosines[pl.ds(s * BW, BW), :] = chirp
    ratio_y = (row - lane).astype(F32) / (height / 4.0)
    table_y[...] = (cosines[...] / (1.0 + ratio_y * ratio_y)).astype(BF16)

    density_copy.wait()
    unit = 1.5 / (slices * depth_count)
    strip = 32

    @pl.loop(0, height // strip)
    def _(b):
        here = pl.ds(pl.multiple_of(b * strip, strip), strip)

        def slice_step(z, carry):
            total, trans, glow_sum, lit_sum = carry
            optical = density[z, here, :].astype(F32) * unit
            total = total + optical
            after = jnp.exp(-total)
            own = trans - after
            weight[z, here, :] = own
            glow_sum = glow_sum + own * heat[z, here, :].astype(F32)
            lit_sum = lit_sum + (jnp.exp(optical) - 1.0)
            return total, after, glow_sum, lit_sum

        zero = jnp.zeros((strip, breadth), F32)
        total, _, glow_sum, lit_sum = lax.fori_loop(
            0, slices, slice_step, (zero, jnp.ones_like(zero), zero, zero), unroll=4
        )
        plane[0, here, :] = glow_sum
        plane[1, here, :] = lit_sum
        high = total.astype(BF16).astype(F32)
        plane[2, here, :] = high
        plane[3, here, :] = total - high

    for d in range(depth_count):
        rows_d = [plane[p, d * band : (d + 1) * band, :] for p in range(4)]
        early_out[d] = jnp.concatenate(rows_d, axis=0).astype(BF16)

    @pl.loop(1, depth_count)
    def _(k):
        early_part(k, lax.rem(depth + k, depth_count), depth).start()

    early_in[depth] = early_out[depth]

    screen_x = (row + tile * breadth).astype(F32)
    scale = 64.0 / (HOT * tile_count * BW)

    def build(source):
        for c in range(2):
            info_c = meta[2 * source + c]
            ratio = (screen_x - info_c[1:2, :]) / (tile_count * height / 2.0)
            value = scale * (cosines[...] / (1.0 + ratio * ratio))
            for m in range(across):
                held = jnp.where(info_c[0:1, :] == float(m * BW), value, 0.0)
                tables[source, m * breadth : (m + 1) * breadth, c * breadth : (c + 1) * breadth] = held.astype(BF16)

    def product(source, q):
        left = jnp.concatenate([blocks[2 * source, q], blocks[2 * source + 1, q]], axis=1)
        return lax.dot_general(left, tables[source], (((1,), (1,)), ((), ())), preferred_element_type=F32)

    def meet(group):
        meta_part(lax.rem(tile - group + tile_count, tile_count), group).wait_recv()

    meet(sibling)
    build(chip)

    @pl.loop(0, QUARTERS)
    def _(q):
        own_part(q, sibling).wait_recv()
        spread[q] = product(chip, q)

    def collect(n):
        for sign in (-1, 1):
            hand_over(n, sign, False).wait_recv()
            source, quarter = arrival(n, sign)
            spread[quarter] += product(source, quarter)

    def finish(q, running):
        def two(i, held):
            mats = []
            for e in range(2):
                lines = spread[q, pl.ds(pl.multiple_of((2 * i + e) * BW, BW), BW), :].astype(BF16)
                mats.append(
                    jnp.concatenate([lines[:, m * breadth : (m + 1) * breadth] for m in range(across)], axis=0)
                )
            inscatter = jnp.dot(table_y[...], jnp.concatenate(mats, axis=1), preferred_element_type=F32)
            z = q * zq + 2 * i
            return held + weight[z] * inscatter[:, :breadth] + weight[z + 1] * inscatter[:, breadth:]

        return lax.fori_loop(0, zq // 2, two, running)

    plane[0] = jnp.zeros((height, breadth), F32)

    @pl.loop(0, steps)
    def _(n):
        for sign in (-1, 1):
            received(n, sign).wait_recv()

            @pl.when(n + 2 < steps)
            def _():
                send(n + 2, sign).start()

            hand_over(n, sign, True).start()

        @pl.when(n > 0)
        def _():
            collect(n - 1)

        @pl.when((n < slots) & (lax.rem(n, 2) == 0))
        def _():
            for sign in (-1, 1):
                source, _ = arrival(n, sign)

                def prepare():
                    meet(2 * source)
                    meet(2 * source + 1)
                    build(source)

                if sign < 0:
                    prepare()
                else:
                    pl.when(n < slots - 1)(prepare)

        @pl.when((n == slots + 1) | (n == slots + 2))
        def _():
            plane[0] = finish(n - slots - 1, plane[0])

        @pl.when(n == slots)
        def _():
            @pl.loop(1, depth_count)
            def _(k):
                early_part(k, depth, lax.rem(depth - k + depth_count, depth_count)).wait_recv()

            def pixel_step(k, carry):
                depth_sum, glow_sum, lit_sum = carry
                held = early_in[k].astype(F32)
                ahead = jnp.exp(-depth_sum)
                before[k] = ahead
                glow_sum = glow_sum + ahead * held[0:band]
                lit_sum = lit_sum + held[band : 2 * band]
                return depth_sum + held[2 * band : 3 * band] + held[3 * band : 4 * band], glow_sum, lit_sum

            zero = jnp.zeros((band, breadth), F32)
            depth_sum, glow_sum, lit_sum = lax.fori_loop(0, depth_count, pixel_step, (zero, zero, zero))
            passed = jnp.exp(-depth_sum)
            base[0] = glow_sum
            base[1] = lit_sum * passed
            base[2] = 1.0 - passed

    collect(steps - 1)
    running = finish(3, finish(2, plane[0]))
    for d in range(depth_count):
        late_out[d] = running[d * band : (d + 1) * band, :]

    @pl.loop(1, depth_count)
    def _(k):
        late_part(k, lax.rem(depth + k, depth_count), depth).start()

    late_in[depth] = late_out[depth]

    @pl.loop(0, steps)
    def _(n):
        for sign in (-1, 1):
            send(n, sign).wait_send()
            hand_over(n, sign, True).wait_send()

    @pl.loop(0, QUARTERS)
    def _(q):
        own_part(q, tile).wait_send()

    @pl.loop(1, tile_count)
    def _(k):
        meta_part(k, tile).wait_send()

    @pl.loop(1, depth_count)
    def _(k):
        early_part(k, lax.rem(depth + k, depth_count), depth).wait_send()

    @pl.loop(1, depth_count)
    def _(k):
        late_part(k, depth, lax.rem(depth - k + depth_count, depth_count)).wait_recv()

    scattered = lax.fori_loop(
        0, depth_count, lambda k, held: held + before[k] * late_in[k], jnp.zeros((band, breadth), F32)
    )
    lit = base[1] + scattered
    for c in range(3):
        out_ref[c] = emit[c] * base[0] + albedo[c] * lit
    out_ref[3] = base[2]

    @pl.loop(1, depth_count)
    def _(k):
        late_part(k, lax.rem(depth + k, depth_count), depth).wait_send()


def shards(density, heat, emit_color, albedo, hot_order, hot_count):
    depth_count = lax.axis_size("depth")
    tile_count = lax.axis_size("tile")
    slices, height, breadth = density.shape
    chips = tile_count // 2
    steps = 2 * (chips - 1)
    rows = slices // QUARTERS * BW
    band = height // depth_count
    across = height // BW
    dma = pltpu.SemaphoreType.DMA
    anywhere = pl.BlockSpec(memory_space=pl.ANY)
    scalars = pl.BlockSpec(memory_space=pltpu.SMEM)
    image = pl.pallas_call(
        functools.partial(render, depth_count, tile_count),
        out_shape=jax.ShapeDtypeStruct((4, band, breadth), F32),
        in_specs=[anywhere, anywhere, scalars, scalars, scalars, scalars],
        out_specs=pl.BlockSpec(memory_space=pltpu.VMEM),
        scratch_shapes=[
            pltpu.VMEM((slices, height, breadth), BF16),
            pltpu.VMEM((slices, height, breadth), BF16),
            pltpu.VMEM((slices, height, breadth), F32),
            pltpu.VMEM((tile_count, QUARTERS, rows, breadth), BF16),
            pltpu.VMEM((QUARTERS, rows, across * breadth), F32),
            pltpu.VMEM((chips, across * breadth, 2 * breadth), BF16),
            pltpu.VMEM((height, breadth), F32),
            pltpu.VMEM((height, breadth), BF16),
            pltpu.VMEM((tile_count, 8, breadth), F32),
            pltpu.VMEM((4, height, breadth), F32),
            pltpu.VMEM((depth_count, 4 * band, breadth), BF16),
            pltpu.VMEM((depth_count, 4 * band, breadth), BF16),
            pltpu.VMEM((depth_count, band, breadth), F32),
            pltpu.VMEM((depth_count, band, breadth), F32),
            pltpu.VMEM((depth_count, band, breadth), F32),
            pltpu.VMEM((3, band, breadth), F32),
            dma((2,)),
            dma((QUARTERS,)), dma((QUARTERS,)),
            dma((steps,)), dma((steps,)), dma((steps,)), dma((steps,)),
            dma((steps,)), dma((steps,)), dma((steps,)), dma((steps,)),
            dma((tile_count,)), dma((tile_count,)),
            dma((depth_count,)), dma((depth_count,)),
            dma((depth_count,)), dma((depth_count,)),
        ],
        compiler_params=pltpu.CompilerParams(
            collective_id=0, has_side_effects=True, vmem_limit_bytes=40 * 1024 * 1024
        ),
        cost_estimate=pl.CostEstimate(flops=3 * 10**9, bytes_accessed=2 * 1024 * 1024, transcendentals=10**6),
    )(density, heat, emit_color, albedo, hot_order, hot_count)
    return image.reshape(4, 1, band * breadth)


def solution(mesh):
    placed = (
        P("depth", None, "tile"),
        P("depth", None, "tile"),
        P(),
        P(),
        P("tile", None),
        P("tile"),
    )
    return jax.shard_map(
        shards, mesh=mesh, in_specs=placed, out_specs=P(None, "tile", "depth"), check_vma=False
    )
```

time: 454 us -> 62.2 us (0.14)
  the two profiles are of different devices: /device:TPU:8 before, /device:TPU:1 now
where the time goes in v1:
time: 62.2 us; the launch traced here: 62 us
  Pallas kernels  58.2 us (94%)
  local copies, waits for them, and re-layouts  3.05 us (5%)
  between operations  0.74 us (1%)
    pallas_call x1, Pallas kernels, shards(): pl.pallas_call(functools.partial(render, depth_count, tile_count), out_sh...  58.2 us
    unnamed x11, local copies, waits for them, and re-layouts  3.05 us

profile of v1, /device:TPU:1, one launch (start us, length us, event | category | flops | bytes accessed | tf_op | source)
XLA Modules:
  0.0 62.0 jit_solution(15061637448266660553)
XLA Ops:
  0.0 0.0 copy-start.4
  0.0 0.0 copy-start.3
  0.0 0.0 copy-start.2
  0.7 0.0 copy-done.4
  0.7 0.0 copy-done.3
  0.7 0.0 copy-done.2
  0.7 0.0 copy-start
  0.7 1.2 %copy-done = bf16[32,128,128]{2,1,0:T(8,128)(2,1)S(1)} copy-done((bf16[32,128,128]{2,1,0:T(8,128)(2,1)S(1)}, bf16[32,128,128]{2,1,0:T(8,128)(2,1)}, u32[]{:S(2)}) %copy-start) | copy-done | bytes 1048600
  2.0 0.0 copy-start.1
  2.0 1.2 %copy-done.1 = bf16[32,128,128]{2,1,0:T(8,128)(2,1)S(1)} copy-done((bf16[32,128,128]{2,1,0:T(8,128)(2,1)S(1)}, bf16[32,128,128]{2,1,0:T(8,128)(2,1)}, u32[]{:S(2)}) %copy-start.1) | copy-done | bytes 1048600
  3.2 58.2 %shard_map.64 = f32[4,4,128]{2,1,0:T(4,128)S(1)} custom-call(bf16[32,128,128]{2,1,0:T(8,128)(2,1)S(1)} %copy-done, bf16[32,128,128]{2,1,0:T(8,128)(2,1)S(1)} %copy-done.1, f32[3]{0:T(128)S(1)} %copy-done.2, f32[3]{0:T(128)S(1)} %copy-done.3, s32[1,16]{1,0:T(1,128)S(1)} %copy-done.4, s32[1]{0:T(128)S(6)} %copy.9.count), custom_call_target="tpu_custom_call" | custom-call | flops 3000000000 | bytes 2097152 | tf_op jit(solution)/shard_map/pallas_call | solution.py:377
  61.4 0.6 copy.10
Async XLA Ops:
  0.0 0.7 %copy-start.4 = (s32[1,16]{1,0:T(1,128)S(1)}, s32[1,16]{1,0:T(1,128)}, u32[]{:S(2)}) copy-start(s32[1,16]{1,0:T(1,128)} %order.1) | copy-start | bytes 196
  0.0 0.7 %copy-start.3 = (f32[3]{0:T(128)S(1)}, f32[3]{0:T(128)}, u32[]{:S(2)}) copy-start(f32[3]{0:T(128)} %albedo.1) | copy-start | bytes 40
  0.0 0.7 %copy-start.2 = (f32[3]{0:T(128)S(1)}, f32[3]{0:T(128)}, u32[]{:S(2)}) copy-start(f32[3]{0:T(128)} %emit.1) | copy-start | bytes 40
  0.7 1.2 %copy-start = (bf16[32,128,128]{2,1,0:T(8,128)(2,1)S(1)}, bf16[32,128,128]{2,1,0:T(8,128)(2,1)}, u32[]{:S(2)}) copy-start(bf16[32,128,128]{2,1,0:T(8,128)(2,1)} %density_hbm.1) | copy-start | bytes 3145732
  2.0 1.2 %copy-start.1 = (bf16[32,128,128]{2,1,0:T(8,128)(2,1)S(1)}, bf16[32,128,128]{2,1,0:T(8,128)(2,1)}, u32[]{:S(2)}) copy-start(bf16[32,128,128]{2,1,0:T(8,128)(2,1)} %heat_hbm.1) | copy-start | bytes 3145732

commit v2 on v1

v2 whole, which is shorter than its diff:
```python
import functools
import math

import jax
import jax.numpy as jnp
from jax import lax
from jax.experimental import pallas as pl
from jax.experimental.pallas import tpu as pltpu
from jax.sharding import PartitionSpec as P

BW = 32
HOT = 4
QUARTERS = 4
HEAD = 16
F32 = jnp.float32
BF16 = jnp.bfloat16
MESH = pl.DeviceIdType.MESH


def iota(shape, axis):
    return lax.broadcasted_iota(jnp.int32, shape, axis)


def render(
    depth_count, tile_count,
    density_hbm, heat_hbm, emit, albedo, order, count,
    out_ref,
    density, heat, weight, blocks, spread, tables, cosines, table_y, plane,
    early_out, early_in, late_out, late_in, before, base,
    heat_sem, density_sem, own_send, own_recv, right_send, right_recv, left_send, left_recv,
    pair_right_send, pair_right_recv, pair_left_send, pair_left_recv,
    early_send, early_recv, late_send, late_recv,
):
    slices, height, breadth = density.shape
    chips = tile_count // 2
    steps = 2 * (chips - 1)
    zq = slices // QUARTERS
    rows = zq * BW
    band = height // depth_count
    depth = lax.axis_index("depth")
    tile = lax.axis_index("tile")
    chip = lax.div(tile, 2)
    core = tile - 2 * chip
    sibling = 2 * chip + 1 - core

    def turned(index, count):
        return jnp.where(index >= count, index - count, index)

    ring = [turned(chip + k, chips) for k in range(chips)]

    def at_tile(index):
        return (depth, index)

    def remote(src, dst, send, recv, device):
        return pltpu.make_async_remote_copy(
            src_ref=src, dst_ref=dst, send_sem=send, recv_sem=recv, device_id=device, device_id_type=MESH
        )

    def fetch(q):
        part = pl.ds(q * zq, zq)
        return (
            pltpu.make_async_copy(heat_hbm.at[part], heat.at[part], heat_sem.at[q]),
            pltpu.make_async_copy(density_hbm.at[part], density.at[part], density_sem.at[q]),
        )

    for q in range(QUARTERS):
        fetch(q)[0].start()
    for q in range(QUARTERS):
        fetch(q)[1].start()

    barrier = pltpu.get_barrier_semaphore()

    @pl.loop(1, tile_count)
    def _(k):
        pl.semaphore_signal(barrier, inc=1, device_id=at_tile(turned(tile + k, tile_count)), device_id_type=MESH)

    @pl.loop(1, depth_count)
    def _(k):
        pl.semaphore_signal(barrier, inc=1, device_id=(turned(depth + k, depth_count), tile), device_id_type=MESH)

    across = height // BW
    lane = iota((height, breadth), 1)
    row = iota((height, breadth), 0)
    lane_h = iota((HEAD, breadth), 1)
    row_h = iota((HEAD, breadth), 0)
    lead = iota((across * breadth, breadth), 0) - iota((across * breadth, breadth), 1) % BW
    slot_of = iota((across * breadth, breadth), 1) // BW
    place = jnp.zeros((across * breadth, breadth), jnp.int32)
    info = jnp.zeros((HEAD, breadth), jnp.int32)
    for s in range(HOT):
        brick = order[0, s]
        x0 = lax.rem(brick, across) * BW
        y0 = lax.div(brick, across) * BW
        dead = 1 - jnp.minimum(jnp.maximum(count[0] - s, 0), 1)
        first = lax.div(brick, across) * breadth + x0 + dead * (2 * across * breadth)
        place = jnp.where(slot_of == s, first, place)
        value = jnp.where(row_h == 0, y0, x0 + lane_h % BW)
        info = jnp.where(lane_h // BW == s, value, info)
    pick = jnp.where(lead == place, 1.0, 0.0).astype(BF16)
    blocks[tile, 0:HEAD, :] = info.astype(F32).astype(BF16)

    def pack(q):
        fetch(q)[0].wait()
        pieces = [
            heat[q * zq : (q + 1) * zq, m * BW : (m + 1) * BW, :].reshape(rows, breadth) for m in range(across)
        ]
        packed = jnp.dot(jnp.concatenate(pieces, axis=1), pick, preferred_element_type=F32)
        blocks[tile, HEAD + q * rows : HEAD + (q + 1) * rows, :] = packed.astype(BF16)

    pack(0)
    pl.semaphore_wait(barrier, tile_count + depth_count - 2)

    half = chips // 2
    order_of = {-1: [0, 1, 2, 3] * (half - 1) + [0, 1], 1: [0, 2, 3, 1] * (half - 1) + [2, 3]}

    def lines(q):
        return pl.ds(0, HEAD + rows) if q == 0 else pl.ds(HEAD + q * rows, rows)

    def block(group, q):
        return blocks.at[group, lines(q)]

    def ring_part(n, sign, source, device):
        sends, recvs = (right_send, right_recv) if sign < 0 else (left_send, left_recv)
        ref = block(2 * source + core, order_of[sign][n])
        return remote(ref, ref, sends.at[n], recvs.at[n], at_tile(device))

    def send(n, sign):
        return ring_part(n, sign, ring[sign * (n // QUARTERS)], 2 * ring[-sign] + core)

    def arrival(n, sign):
        return ring[sign * (n // QUARTERS + 1)], order_of[sign][n]

    def received(n, sign):
        return ring_part(n, sign, arrival(n, sign)[0], sibling)

    def onward(n, sign):
        later = [m for m in range(n + 1, steps) if m // QUARTERS == n // QUARTERS + 1]
        return [m for m in later if order_of[sign][m] == order_of[sign][n]]

    def hand_over(n, sign, mine):
        source, quarter = arrival(n, sign)
        sends, recvs = (pair_right_send, pair_right_recv) if sign < 0 else (pair_left_send, pair_left_recv)
        ref = block(2 * source + (core if mine else 1 - core), quarter)
        return remote(ref, ref, sends.at[n], recvs.at[n], at_tile(sibling))

    def own_part(q, group):
        ref = block(group, q)
        return remote(ref, ref, own_send.at[q], own_recv.at[q], at_tile(sibling))

    def early_part(k, target, source):
        return remote(
            early_out.at[target], early_in.at[source], early_send.at[k], early_recv.at[k], (target, tile)
        )

    def late_part(k, target, source):
        return remote(late_out.at[target], late_in.at[source], late_send.at[k], late_recv.at[k], (target, tile))

    for q in range(QUARTERS):
        if q > 0:
            pack(q)
        for sign in (-1, 1):
            for n in range(QUARTERS):
                if max(order_of[sign][: n + 1]) == q and (order_of[sign][n] == q or n == QUARTERS - 1):
                    send(n, sign).start()
        own_part(q, tile).start()

    offset = iota((BW, breadth), 0) - iota((BW, breadth), 1)
    turn = (offset * offset) % (2 * BW)
    chirp = jnp.cos(turn.astype(F32) * (math.pi / BW) + math.pi / 8.0)
    for s in range(height // BW):
        cosines[pl.ds(s * BW, BW), :] = chirp
    ratio_y = (row - lane).astype(F32) / (height / 4.0)
    table_y[...] = (cosines[...] / (1.0 + ratio_y * ratio_y)).astype(BF16)

    for q in range(QUARTERS):
        fetch(q)[1].wait()
    unit = 1.5 / (slices * depth_count)
    strip = 32

    @pl.loop(0, height // strip)
    def _(b):
        here = pl.ds(pl.multiple_of(b * strip, strip), strip)

        def slice_step(z, carry):
            total, trans, glow_sum, lit_sum = carry
            optical = density[z, here, :].astype(F32) * unit
            total = total + optical
            after = jnp.exp(-total)
            own = trans - after
            weight[z, here, :] = own
            glow_sum = glow_sum + own * heat[z, here, :].astype(F32)
            lit_sum = lit_sum + (jnp.exp(optical) - 1.0)
            return total, after, glow_sum, lit_sum

        zero = jnp.zeros((strip, breadth), F32)
        total, _, glow_sum, lit_sum = lax.fori_loop(
            0, slices, slice_step, (zero, jnp.ones_like(zero), zero, zero), unroll=4
        )
        plane[0, here, :] = glow_sum
        plane[1, here, :] = lit_sum
        high = total.astype(BF16).astype(F32)
        plane[2, here, :] = high
        plane[3, here, :] = total - high

    for d in range(depth_count):
        rows_d = [plane[p, d * band : (d + 1) * band, :] for p in range(4)]
        early_out[d] = jnp.concatenate(rows_d, axis=0).astype(BF16)

    @pl.loop(1, depth_count)
    def _(k):
        early_part(k, turned(depth + k, depth_count), depth).start()

    early_in[depth] = early_out[depth]

    scale = 64.0 / (HOT * tile_count * BW)

    def build(source):
        for c in range(2):
            info_c = blocks[2 * source + c, 0:HEAD, :].astype(F32).T
            shift = ((tile - 2 * source - c) * breadth).astype(F32)
            ratio = (lane.astype(F32) + shift - info_c[:, 1:2]) / (tile_count * height / 2.0)
            value = scale * (cosines[...] / (1.0 + ratio * ratio))
            for m in range(across):
                held = jnp.where(info_c[:, 0:1] == float(m * BW), value, 0.0)
                tables[source, c * breadth : (c + 1) * breadth, m * breadth : (m + 1) * breadth] = held.astype(BF16)

    def product(source, q):
        part = slice(HEAD + q * rows, HEAD + (q + 1) * rows)
        left = jnp.concatenate([blocks[2 * source, part, :], blocks[2 * source + 1, part, :]], axis=1)
        return jnp.dot(left, tables[source], preferred_element_type=F32)

    own_part(0, sibling).wait_recv()
    build(chip)
    spread[0] = product(chip, 0)
    for q in range(1, QUARTERS):
        own_part(q, sibling).wait_recv()
        spread[q] = product(chip, q)

    def collect(n):
        for sign in (-1, 1):
            hand_over(n, sign, False).wait_recv()
        for sign in (-1, 1):
            source, quarter = arrival(n, sign)
            if quarter == 0:
                build(source)
            spread[quarter] += product(source, quarter)

    def finish(q, running):
        mats = []
        for z in range(zq):
            flat = spread[q, z * BW : (z + 1) * BW, :].astype(BF16)
            mats.append(jnp.concatenate([flat[:, m * breadth : (m + 1) * breadth] for m in range(across)], axis=0))
        inscatter = jnp.dot(table_y[...], jnp.concatenate(mats, axis=1), preferred_element_type=F32)
        for z in range(zq):
            running = running + weight[q * zq + z] * inscatter[:, z * breadth : (z + 1) * breadth]
        return running

    def gather_early():
        @pl.loop(1, depth_count)
        def _(k):
            early_part(k, depth, turned(depth - k + depth_count, depth_count)).wait_recv()

        def pixel_step(k, carry):
            depth_sum, glow_sum, lit_sum = carry
            held = early_in[k].astype(F32)
            ahead = jnp.exp(-depth_sum)
            before[k] = ahead
            glow_sum = glow_sum + ahead * held[0:band]
            lit_sum = lit_sum + held[band : 2 * band]
            return depth_sum + held[2 * band : 3 * band] + held[3 * band : 4 * band], glow_sum, lit_sum

        zero = jnp.zeros((band, breadth), F32)
        depth_sum, glow_sum, lit_sum = lax.fori_loop(0, depth_count, pixel_step, (zero, zero, zero))
        passed = jnp.exp(-depth_sum)
        base[0] = glow_sum
        base[1] = lit_sum * passed
        base[2] = 1.0 - passed

    for n in range(steps):
        for sign in (-1, 1):
            received(n, sign).wait_recv()
            for m in onward(n, sign):
                send(m, sign).start()
            hand_over(n, sign, True).start()
        if n > 0:
            collect(n - 1)
        if n == 2 * half:
            gather_early()

    running = finish(2, finish(0, jnp.zeros((height, breadth), F32)))
    collect(steps - 1)
    running = finish(3, finish(1, running))
    for d in range(depth_count):
        late_out[d] = running[d * band : (d + 1) * band, :]

    @pl.loop(1, depth_count)
    def _(k):
        late_part(k, turned(depth + k, depth_count), depth).start()

    late_in[depth] = late_out[depth]

    for n in range(steps):
        for sign in (-1, 1):
            send(n, sign).wait_send()
            hand_over(n, sign, True).wait_send()

    for q in range(QUARTERS):
        own_part(q, tile).wait_send()

    @pl.loop(1, depth_count)
    def _(k):
        early_part(k, turned(depth + k, depth_count), depth).wait_send()

    @pl.loop(1, depth_count)
    def _(k):
        late_part(k, depth, turned(depth - k + depth_count, depth_count)).wait_recv()

    scattered = lax.fori_loop(
        0, depth_count, lambda k, held: held + before[k] * late_in[k], jnp.zeros((band, breadth), F32)
    )
    lit = base[1] + scattered
    for c in range(3):
        out_ref[c] = emit[c] * base[0] + albedo[c] * lit
    out_ref[3] = base[2]

    @pl.loop(1, depth_count)
    def _(k):
        late_part(k, turned(depth + k, depth_count), depth).wait_send()


def shards(density, heat, emit_color, albedo, hot_order, hot_count):
    depth_count = lax.axis_size("depth")
    tile_count = lax.axis_size("tile")
    slices, height, breadth = density.shape
    chips = tile_count // 2
    steps = 2 * (chips - 1)
    rows = slices // QUARTERS * BW
    band = height // depth_count
    across = height // BW
    dma = pltpu.SemaphoreType.DMA
    anywhere = pl.BlockSpec(memory_space=pltpu.HBM)
    scalars = pl.BlockSpec(memory_space=pltpu.SMEM)
    image = pl.pallas_call(
        functools.partial(render, depth_count, tile_count),
        out_shape=jax.ShapeDtypeStruct((4, band, breadth), F32),
        in_specs=[anywhere, anywhere, scalars, scalars, scalars, scalars],
        out_specs=pl.BlockSpec(memory_space=pltpu.VMEM),
        scratch_shapes=[
            pltpu.VMEM((slices, height, breadth), BF16),
            pltpu.VMEM((slices, height, breadth), BF16),
            pltpu.VMEM((slices, height, breadth), F32),
            pltpu.VMEM((tile_count, HEAD + slices * BW, breadth), BF16),
            pltpu.VMEM((QUARTERS, rows, across * breadth), F32),
            pltpu.VMEM((chips, 2 * breadth, across * breadth), BF16),
            pltpu.VMEM((height, breadth), F32),
            pltpu.VMEM((height, breadth), BF16),
            pltpu.VMEM((4, height, breadth), F32),
            pltpu.VMEM((depth_count, 4 * band, breadth), BF16),
            pltpu.VMEM((depth_count, 4 * band, breadth), BF16),
            pltpu.VMEM((depth_count, band, breadth), F32),
            pltpu.VMEM((depth_count, band, breadth), F32),
            pltpu.VMEM((depth_count, band, breadth), F32),
            pltpu.VMEM((3, band, breadth), F32),
            dma((QUARTERS,)), dma((QUARTERS,)),
            dma((QUARTERS,)), dma((QUARTERS,)),
            dma((steps,)), dma((steps,)), dma((steps,)), dma((steps,)),
            dma((steps,)), dma((steps,)), dma((steps,)), dma((steps,)),
            dma((depth_count,)), dma((depth_count,)),
            dma((depth_count,)), dma((depth_count,)),
        ],
        compiler_params=pltpu.CompilerParams(
            collective_id=0, has_side_effects=True, vmem_limit_bytes=60 * 1024 * 1024
        ),
        cost_estimate=pl.CostEstimate(flops=3 * 10**9, bytes_accessed=2 * 1024 * 1024, transcendentals=10**6),
    )(density, heat, emit_color, albedo, hot_order, hot_count)
    return image.reshape(4, 1, band * breadth)


def solution(mesh):
    placed = (
        P("depth", None, "tile"),
        P("depth", None, "tile"),
        P(),
        P(),
        P("tile", None),
        P("tile"),
    )
    return jax.shard_map(
        shards, mesh=mesh, in_specs=placed, out_specs=P(None, "tile", "depth"), check_vma=False
    )
```

time: 62.2 us -> 51.1 us (0.82)
  Pallas kernels: 58.2 us -> 49 us
  local copies, waits for them, and re-layouts: 3.05 us -> 1.3 us
    pallas_call x1, Pallas kernels: 58.2 us -> 49 us  [shards(): pl.pallas_call(functools.partial(render, depth_count, tile_count), out_sh...]
    unnamed x11 -> x1, local copies, waits for them, and re-layouts: 3.05 us -> 1.3 us
where the time goes in v2:
time: 51.1 us; the launch traced here: 51 us
  Pallas kernels  49 us (96%)
  local copies, waits for them, and re-layouts  1.3 us (3%)
  between operations  0.66 us (1%)
    pallas_call x1, Pallas kernels, shards(): pl.pallas_call(functools.partial(render, depth_count, tile_count), out_sh...  49 us
    unnamed x1, local copies, waits for them, and re-layouts  1.3 us

profile of v2, /device:TPU:1, one launch (start us, length us, event | category | flops | bytes accessed | tf_op | source)
XLA Modules:
  0.0 51.0 jit_solution(4826530145600300685)
XLA Ops:
  0.7 49.0 %shard_map.64 = f32[4,4,128]{2,1,0:T(4,128)} custom-call(bf16[32,128,128]{2,1,0:T(8,128)(2,1)} %density_hbm.1, bf16[32,128,128]{2,1,0:T(8,128)(2,1)} %heat_hbm.1, f32[3]{0:T(128)} %emit.1, f32[3]{0:T(128)} %albedo.1, s32[1,16]{1,0:T(1,128)} %order.1, s32[1]{0:T(128)S(6)} %copy.9.count), custom_call_target="tpu_custom_call" | custom-call | flops 3000000000 | bytes 2097152 | tf_op jit(solution)/shard_map/pallas_call | solution.py:343
  49.7 1.3 %copy.10 = f32[4,1,512]{2,1,0:T(1,128)} copy(f32[4,1,512]{2,1,0:T(1,128)} %bitcast.1) | data formatting | bytes 16384

commit v3 on v2

--- a/solution.py
+++ b/solution.py
@@ -12,6 +12,7 @@
 HOT = 4
 QUARTERS = 4
 HEAD = 16
+COLUMNS = 4
 F32 = jnp.float32
 BF16 = jnp.bfloat16
 MESH = pl.DeviceIdType.MESH
@@ -23,13 +24,13 @@
 
 def render(
     depth_count, tile_count,
-    density_hbm, heat_hbm, emit, albedo, order, count,
+    density_hbm, heat_hbm, emit_hbm, albedo_hbm, order_hbm, count_hbm,
     out_ref,
-    density, heat, weight, blocks, spread, tables, cosines, table_y, plane,
+    emit, albedo, order, count, density, heat, weight, blocks, spread, tables, cosines, table_y, plane,
     early_out, early_in, late_out, late_in, before, base,
-    heat_sem, density_sem, own_send, own_recv, right_send, right_recv, left_send, left_recv,
+    scalar_sem, heat_sem, density_sem, own_send, own_recv, right_send, right_recv, left_send, left_recv,
     pair_right_send, pair_right_recv, pair_left_send, pair_left_recv,
-    early_send, early_recv, late_send, late_recv,
+    early_send, early_recv, late_send, late_recv, word,
 ):
     slices, height, breadth = density.shape
     chips = tile_count // 2
@@ -47,6 +48,25 @@
         return jnp.where(index >= count, index - count, index)
 
     ring = [turned(chip + k, chips) for k in range(chips)]
+    columns = min(COLUMNS, depth_count)
+    planes = depth_count // columns
+    z_here = lax.div(depth, columns)
+    x_here = depth - z_here * columns
+    z_ring = [turned(z_here + k, planes) for k in range(planes)]
+    x_ring = [turned(x_here + k, columns) for k in range(columns)]
+
+    def beside(size):
+        return [1, size - 1] if size > 2 else [1] * (size - 1)
+
+    x_beside = [(z_here * columns + x_ring[k], tile) for k in beside(columns)]
+    z_beside = [(z_ring[k] * columns + x_here, tile) for k in beside(planes)]
+    far_first = sorted(
+        [(a, b) for a in range(planes) for b in range(columns) if a + b],
+        key=lambda e: -min(e[0], planes - e[0]) - min(e[1], columns - e[1]),
+    )
+
+    def partner(a, b):
+        return z_ring[a] * columns + x_ring[b]
 
     def at_tile(index):
         return (depth, index)
@@ -63,20 +83,33 @@
             pltpu.make_async_copy(density_hbm.at[part], density.at[part], density_sem.at[q]),
         )
 
-    for q in range(QUARTERS):
+    scalars = [(order_hbm, order), (count_hbm, count), (emit_hbm, emit), (albedo_hbm, albedo)]
+    loads = [pltpu.make_async_copy(src, dst, scalar_sem.at[i]) for i, (src, dst) in enumerate(scalars)]
+    loads[0].start()
+    loads[1].start()
+    fetch(0)[0].start()
+
+    barrier = pltpu.get_barrier_semaphore()
+
+    greeted = [(depth, 2 * ring[1] + core), (depth, 2 * ring[-1] + core), (depth, sibling)] + x_beside + z_beside
+    for device in greeted:
+        pl.semaphore_signal(barrier, inc=1, device_id=device, device_id_type=MESH)
+
+    for q in range(1, QUARTERS):
         fetch(q)[0].start()
     for q in range(QUARTERS):
         fetch(q)[1].start()
-
-    barrier = pltpu.get_barrier_semaphore()
-
-    @pl.loop(1, tile_count)
-    def _(k):
-        pl.semaphore_signal(barrier, inc=1, device_id=at_tile(turned(tile + k, tile_count)), device_id_type=MESH)
-
-    @pl.loop(1, depth_count)
-    def _(k):
-        pl.semaphore_signal(barrier, inc=1, device_id=(turned(depth + k, depth_count), tile), device_id_type=MESH)
+    loads[2].start()
+    loads[3].start()
+
+    rounds = [x_beside] * (columns // 2 - 1) + [z_beside] * (planes // 2)
+
+    def pass_word(r):
+        if 0 < r <= len(rounds):
+            pl.semaphore_wait(word.at[r - 1], len(rounds[r - 1]))
+        if r < len(rounds):
+            for device in rounds[r]:
+                pl.semaphore_signal(word.at[r], inc=1, device_id=device, device_id_type=MESH)
 
     across = height // BW
     lane = iota((height, breadth), 1)
@@ -87,6 +120,8 @@
     slot_of = iota((across * breadth, breadth), 1) // BW
     place = jnp.zeros((across * breadth, breadth), jnp.int32)
     info = jnp.zeros((HEAD, breadth), jnp.int32)
+    loads[0].wait()
+    loads[1].wait()
     for s in range(HOT):
         brick = order[0, s]
         x0 = lax.rem(brick, across) * BW
@@ -108,7 +143,7 @@
         blocks[tile, HEAD + q * rows : HEAD + (q + 1) * rows, :] = packed.astype(BF16)
 
     pack(0)
-    pl.semaphore_wait(barrier, tile_count + depth_count - 2)
+    pl.semaphore_wait(barrier, len(greeted))
 
     half = chips // 2
     order_of = {-1: [0, 1, 2, 3] * (half - 1) + [0, 1], 1: [0, 2, 3, 1] * (half - 1) + [2, 3]}
@@ -147,13 +182,21 @@
         ref = block(group, q)
         return remote(ref, ref, own_send.at[q], own_recv.at[q], at_tile(sibling))
 
-    def early_part(k, target, source):
+    def early_part(a, b, target, source):
+        k = a * columns + b
         return remote(
             early_out.at[target], early_in.at[source], early_send.at[k], early_recv.at[k], (target, tile)
         )
 
-    def late_part(k, target, source):
+    def late_part(a, b, target, source):
+        k = a * columns + b
         return remote(late_out.at[target], late_in.at[source], late_send.at[k], late_recv.at[k], (target, tile))
+
+    def leaving(part, a, b):
+        return part(a, b, partner(a, b), depth)
+
+    def coming(part, a, b):
+        return part(a, b, depth, partner(-a, -b))
 
     for q in range(QUARTERS):
         if q > 0:
@@ -163,6 +206,7 @@
                 if max(order_of[sign][: n + 1]) == q and (order_of[sign][n] == q or n == QUARTERS - 1):
                     send(n, sign).start()
         own_part(q, tile).start()
+    pass_word(0)
 
     offset = iota((BW, breadth), 0) - iota((BW, breadth), 1)
     turn = (offset * offset) % (2 * BW)
@@ -206,10 +250,6 @@
         rows_d = [plane[p, d * band : (d + 1) * band, :] for p in range(4)]
         early_out[d] = jnp.concatenate(rows_d, axis=0).astype(BF16)
 
-    @pl.loop(1, depth_count)
-    def _(k):
-        early_part(k, turned(depth + k, depth_count), depth).start()
-
     early_in[depth] = early_out[depth]
 
     scale = 64.0 / (HOT * tile_count * BW)
@@ -256,9 +296,8 @@
         return running
 
     def gather_early():
-        @pl.loop(1, depth_count)
-        def _(k):
-            early_part(k, depth, turned(depth - k + depth_count, depth_count)).wait_recv()
+        for a, b in far_first:
+            coming(early_part, a, b).wait_recv()
 
         def pixel_step(k, carry):
             depth_sum, glow_sum, lit_sum = carry
@@ -284,7 +323,11 @@
             hand_over(n, sign, True).start()
         if n > 0:
             collect(n - 1)
-        if n == 2 * half:
+        pass_word(n + 1)
+        if n + 1 == max(len(rounds), 1):
+            for a, b in far_first:
+                leaving(early_part, a, b).start()
+        if n == steps - 4:
             gather_early()
 
     running = finish(2, finish(0, jnp.zeros((height, breadth), F32)))
@@ -293,9 +336,8 @@
     for d in range(depth_count):
         late_out[d] = running[d * band : (d + 1) * band, :]
 
-    @pl.loop(1, depth_count)
-    def _(k):
-        late_part(k, turned(depth + k, depth_count), depth).start()
+    for a, b in far_first:
+        leaving(late_part, a, b).start()
 
     late_in[depth] = late_out[depth]
 
@@ -307,25 +349,23 @@
     for q in range(QUARTERS):
         own_part(q, tile).wait_send()
 
-    @pl.loop(1, depth_count)
-    def _(k):
-        early_part(k, turned(depth + k, depth_count), depth).wait_send()
-
-    @pl.loop(1, depth_count)
-    def _(k):
-        late_part(k, depth, turned(depth - k + depth_count, depth_count)).wait_recv()
+    for a, b in far_first:
+        leaving(early_part, a, b).wait_send()
+    for a, b in far_first:
+        coming(late_part, a, b).wait_recv()
 
     scattered = lax.fori_loop(
         0, depth_count, lambda k, held: held + before[k] * late_in[k], jnp.zeros((band, breadth), F32)
     )
+    loads[2].wait()
+    loads[3].wait()
     lit = base[1] + scattered
     for c in range(3):
         out_ref[c] = emit[c] * base[0] + albedo[c] * lit
     out_ref[3] = base[2]
 
-    @pl.loop(1, depth_count)
-    def _(k):
-        late_part(k, turned(depth + k, depth_count), depth).wait_send()
+    for a, b in far_first:
+        leaving(late_part, a, b).wait_send()
 
 
 def shards(density, heat, emit_color, albedo, hot_order, hot_count):
@@ -338,14 +378,14 @@
     band = height // depth_count
     across = height // BW
     dma = pltpu.SemaphoreType.DMA
-    anywhere = pl.BlockSpec(memory_space=pltpu.HBM)
-    scalars = pl.BlockSpec(memory_space=pltpu.SMEM)
+    anywhere = pl.BlockSpec(memory_space=pl.ANY)
     image = pl.pallas_call(
         functools.partial(render, depth_count, tile_count),
         out_shape=jax.ShapeDtypeStruct((4, band, breadth), F32),
-        in_specs=[anywhere, anywhere, scalars, scalars, scalars, scalars],
+        in_specs=[anywhere] * 6,
         out_specs=pl.BlockSpec(memory_space=pltpu.VMEM),
         scratch_shapes=[
+            pltpu.SMEM((3,), F32), pltpu.SMEM((3,), F32), pltpu.SMEM((1, 16), jnp.int32), pltpu.SMEM((1,), jnp.int32),
             pltpu.VMEM((slices, height, breadth), BF16),
             pltpu.VMEM((slices, height, breadth), BF16),
             pltpu.VMEM((slices, height, breadth), F32),
@@ -361,15 +401,16 @@
             pltpu.VMEM((depth_count, band, breadth), F32),
             pltpu.VMEM((depth_count, band, breadth), F32),
             pltpu.VMEM((3, band, breadth), F32),
-            dma((QUARTERS,)), dma((QUARTERS,)),
+            dma((4,)), dma((QUARTERS,)), dma((QUARTERS,)),
             dma((QUARTERS,)), dma((QUARTERS,)),
             dma((steps,)), dma((steps,)), dma((steps,)), dma((steps,)),
             dma((steps,)), dma((steps,)), dma((steps,)), dma((steps,)),
             dma((depth_count,)), dma((depth_count,)),
             dma((depth_count,)), dma((depth_count,)),
+            pltpu.SemaphoreType.REGULAR((8,)),
         ],
         compiler_params=pltpu.CompilerParams(
-            collective_id=0, has_side_effects=True, vmem_limit_bytes=60 * 1024 * 1024
+            collective_id=0, has_side_effects=True, vmem_limit_bytes=54400 * 1024
         ),
         cost_estimate=pl.CostEstimate(flops=3 * 10**9, bytes_accessed=2 * 1024 * 1024, transcendentals=10**6),
     )(density, heat, emit_color, albedo, hot_order, hot_count)

time: 51.1 us -> 46.5 us (0.910)
  Pallas kernels: 49 us -> 45 us
  local copies, waits for them, and re-layouts: 1.3 us -> 0.61 us
    pallas_call x1, Pallas kernels: 49 us -> 45 us  [shards(): pl.pallas_call(functools.partial(render, depth_count, tile_count), out_sh...]
    unnamed x1 -> x7, local copies, waits for them, and re-layouts: 1.3 us -> 0.61 us
where the time goes in v3:
time: 46.5 us; the launch traced here: 46.4 us
  Pallas kernels  45 us (97%)
  between operations  0.73 us (2%)
  local copies, waits for them, and re-layouts  0.61 us (1%)
    pallas_call x1, Pallas kernels, shards(): pl.pallas_call(functools.partial(render, depth_count, tile_count), out_sh...  45 us

profile of v3, /device:TPU:1, one launch (start us, length us, event | category | flops | bytes accessed | tf_op | source)
XLA Modules:
  0.0 46.4 jit_solution(827713226530195012)
XLA Ops:
  0.0 0.0 copy-start.2
  0.0 0.0 copy-start.1
  0.0 0.0 copy-start
  0.7 0.0 copy-done.2
  0.7 0.0 copy-done.1
  0.7 0.0 copy-done
  0.7 45.0 %shard_map.64 = f32[4,4,128]{2,1,0:T(4,128)S(1)} custom-call(bf16[32,128,128]{2,1,0:T(8,128)(2,1)} %density_hbm.1, bf16[32,128,128]{2,1,0:T(8,128)(2,1)} %heat_hbm.1, f32[3]{0:T(128)S(1)} %copy-done, f32[3]{0:T(128)S(1)} %copy-done.1, s32[1,16]{1,0:T(1,128)S(1)} %copy-done.2, s32[1]{0:T(128)S(6)} %copy.9.count_hbm), custom_call_target="tpu_custom_call" | custom-call | flops 3000000000 | bytes 2097152 | tf_op jit(solution)/shard_map/pallas_call | solution.py:382
  45.8 0.6 %copy.10 = f32[4,1,512]{2,1,0:T(1,128)} copy(f32[4,1,512]{2,1,0:T(1,128)S(1)} %bitcast.1) | data formatting | bytes 16384
Async XLA Ops:
  0.0 0.7 %copy-start.2 = (s32[1,16]{1,0:T(1,128)S(1)}, s32[1,16]{1,0:T(1,128)}, u32[]{:S(2)}) copy-start(s32[1,16]{1,0:T(1,128)} %order_hbm.1) | copy-start | bytes 196
  0.0 0.7 %copy-start.1 = (f32[3]{0:T(128)S(1)}, f32[3]{0:T(128)}, u32[]{:S(2)}) copy-start(f32[3]{0:T(128)} %albedo_hbm.1) | copy-start | bytes 40
  0.0 0.7 %copy-start = (f32[3]{0:T(128)S(1)}, f32[3]{0:T(128)}, u32[]{:S(2)}) copy-start(f32[3]{0:T(128)} %emit_hbm.1) | copy-start | bytes 40

commit v4 on v3

--- a/solution.py
+++ b/solution.py
@@ -13,6 +13,7 @@
 QUARTERS = 4
 HEAD = 16
 COLUMNS = 4
+BEHIND = 4
 F32 = jnp.float32
 BF16 = jnp.bfloat16
 MESH = pl.DeviceIdType.MESH
@@ -182,21 +183,21 @@
         ref = block(group, q)
         return remote(ref, ref, own_send.at[q], own_recv.at[q], at_tile(sibling))
 
-    def early_part(a, b, target, source):
-        k = a * columns + b
-        return remote(
-            early_out.at[target], early_in.at[source], early_send.at[k], early_recv.at[k], (target, tile)
-        )
-
-    def late_part(a, b, target, source):
-        k = a * columns + b
-        return remote(late_out.at[target], late_in.at[source], late_send.at[k], late_recv.at[k], (target, tile))
+    def early_part(target, source):
+        return remote(early_out.at[target], early_in.at[source], early_send, early_recv, (target, tile))
+
+    def late_part(target, source):
+        return remote(late_out.at[target], late_in.at[source], late_send, late_recv, (target, tile))
 
     def leaving(part, a, b):
-        return part(a, b, partner(a, b), depth)
-
-    def coming(part, a, b):
-        return part(a, b, depth, partner(-a, -b))
+        return part(partner(a, b), depth)
+
+    def everyone(out, into, send_sem, recv_sem):
+        others = pl.ds(0, depth_count - 1)
+        return remote(out.at[others], into.at[others], send_sem, recv_sem, (depth, sibling))
+
+    early_all = everyone(early_out, early_in, early_send, early_recv)
+    late_all = everyone(late_out, late_in, late_send, late_recv)
 
     for q in range(QUARTERS):
         if q > 0:
@@ -296,33 +297,42 @@
         return running
 
     def gather_early():
-        for a, b in far_first:
-            coming(early_part, a, b).wait_recv()
-
-        def pixel_step(k, carry):
-            depth_sum, glow_sum, lit_sum = carry
+        early_all.wait_recv()
+        early_all.wait_send()
+
+        zero = jnp.zeros((band, breadth), F32)
+        depth_sum, glow_sum, lit_sum = zero, zero, zero
+        for k in range(depth_count):
             held = early_in[k].astype(F32)
             ahead = jnp.exp(-depth_sum)
             before[k] = ahead
             glow_sum = glow_sum + ahead * held[0:band]
             lit_sum = lit_sum + held[band : 2 * band]
-            return depth_sum + held[2 * band : 3 * band] + held[3 * band : 4 * band], glow_sum, lit_sum
-
-        zero = jnp.zeros((band, breadth), F32)
-        depth_sum, glow_sum, lit_sum = lax.fori_loop(0, depth_count, pixel_step, (zero, zero, zero))
+            depth_sum = depth_sum + held[2 * band : 3 * band] + held[3 * band : 4 * band]
         passed = jnp.exp(-depth_sum)
         base[0] = glow_sum
         base[1] = lit_sum * passed
         base[2] = 1.0 - passed
 
+    def settle(n):
+        for sign in (-1, 1):
+            send(n, sign).wait_send()
+            hand_over(n, sign, True).wait_send()
+
     for n in range(steps):
         for sign in (-1, 1):
             received(n, sign).wait_recv()
             for m in onward(n, sign):
                 send(m, sign).start()
+        for sign in (-1, 1):
             hand_over(n, sign, True).start()
-        if n > 0:
-            collect(n - 1)
+        if n >= BEHIND:
+            collect(n - BEHIND)
+        if n >= 2:
+            settle(n - 2)
+        if n == 2:
+            for q in range(QUARTERS):
+                own_part(q, tile).wait_send()
         pass_word(n + 1)
         if n + 1 == max(len(rounds), 1):
             for a, b in far_first:
@@ -330,6 +340,8 @@
         if n == steps - 4:
             gather_early()
 
+    for n in range(steps - BEHIND, steps - 1):
+        collect(n)
     running = finish(2, finish(0, jnp.zeros((height, breadth), F32)))
     collect(steps - 1)
     running = finish(3, finish(1, running))
@@ -341,22 +353,10 @@
 
     late_in[depth] = late_out[depth]
 
-    for n in range(steps):
-        for sign in (-1, 1):
-            send(n, sign).wait_send()
-            hand_over(n, sign, True).wait_send()
-
-    for q in range(QUARTERS):
-        own_part(q, tile).wait_send()
-
-    for a, b in far_first:
-        leaving(early_part, a, b).wait_send()
-    for a, b in far_first:
-        coming(late_part, a, b).wait_recv()
-
-    scattered = lax.fori_loop(
-        0, depth_count, lambda k, held: held + before[k] * late_in[k], jnp.zeros((band, breadth), F32)
-    )
+    for n in range(steps - 2, steps):
+        settle(n)
+    late_all.wait_recv()
+    scattered = jnp.sum(before[...] * late_in[...], axis=0)
     loads[2].wait()
     loads[3].wait()
     lit = base[1] + scattered
@@ -364,8 +364,7 @@
         out_ref[c] = emit[c] * base[0] + albedo[c] * lit
     out_ref[3] = base[2]
 
-    for a, b in far_first:
-        leaving(late_part, a, b).wait_send()
+    late_all.wait_send()
 
 
 def shards(density, heat, emit_color, albedo, hot_order, hot_count):
@@ -405,8 +404,7 @@
             dma((QUARTERS,)), dma((QUARTERS,)),
             dma((steps,)), dma((steps,)), dma((steps,)), dma((steps,)),
             dma((steps,)), dma((steps,)), dma((steps,)), dma((steps,)),
-            dma((depth_count,)), dma((depth_count,)),
-            dma((depth_count,)), dma((depth_count,)),
+            dma, dma, dma, dma,
             pltpu.SemaphoreType.REGULAR((8,)),
         ],
         compiler_params=pltpu.CompilerParams(

time: 46.5 us -> 44.7 us (0.961)
  Pallas kernels: 45 us -> 43.2 us
    pallas_call x1, Pallas kernels: 45 us -> 43.2 us  [shards(): pl.pallas_call(functools.partial(render, depth_count, tile_count), out_sh...]
where the time goes in v4:
time: 44.7 us; the launch traced here: 44.6 us
  Pallas kernels  43.2 us (97%)
  between operations  0.73 us (2%)
  local copies, waits for them, and re-layouts  0.61 us (1%)
    pallas_call x1, Pallas kernels, shards(): pl.pallas_call(functools.partial(render, depth_count, tile_count), out_sh...  43.2 us

profile of v4, /device:TPU:1, one launch (start us, length us, event | category | flops | bytes accessed | tf_op | source)
XLA Modules:
  0.0 44.6 jit_solution(12299740134340934902)
XLA Ops:
  0.0 0.0 copy-start.2
  0.0 0.0 copy-start.1
  0.0 0.0 copy-start
  0.7 0.0 copy-done.2
  0.7 0.0 copy-done.1
  0.7 0.0 copy-done
  0.7 43.2 %shard_map.64 = f32[4,4,128]{2,1,0:T(4,128)S(1)} custom-call(bf16[32,128,128]{2,1,0:T(8,128)(2,1)} %density_hbm.1, bf16[32,128,128]{2,1,0:T(8,128)(2,1)} %heat_hbm.1, f32[3]{0:T(128)S(1)} %copy-done, f32[3]{0:T(128)S(1)} %copy-done.1, s32[1,16]{1,0:T(1,128)S(1)} %copy-done.2, s32[1]{0:T(128)S(6)} %copy.9.count_hbm), custom_call_target="tpu_custom_call" | custom-call | flops 3000000000 | bytes 2097152 | tf_op jit(solution)/shard_map/pallas_call | solution.py:381
  44.0 0.6 %copy.10 = f32[4,1,512]{2,1,0:T(1,128)} copy(f32[4,1,512]{2,1,0:T(1,128)S(1)} %bitcast.1) | data formatting | bytes 16384
Async XLA Ops:
  0.0 0.7 %copy-start.2 = (s32[1,16]{1,0:T(1,128)S(1)}, s32[1,16]{1,0:T(1,128)}, u32[]{:S(2)}) copy-start(s32[1,16]{1,0:T(1,128)} %order_hbm.1) | copy-start | bytes 196
  0.0 0.7 %copy-start.1 = (f32[3]{0:T(128)S(1)}, f32[3]{0:T(128)}, u32[]{:S(2)}) copy-start(f32[3]{0:T(128)} %albedo_hbm.1) | copy-start | bytes 40
  0.0 0.7 %copy-start = (f32[3]{0:T(128)S(1)}, f32[3]{0:T(128)}, u32[]{:S(2)}) copy-start(f32[3]{0:T(128)} %emit_hbm.1) | copy-start | bytes 40

commit v5 on v4

--- a/solution.py
+++ b/solution.py
@@ -13,7 +13,7 @@
 QUARTERS = 4
 HEAD = 16
 COLUMNS = 4
-BEHIND = 4
+BEHIND = 3
 F32 = jnp.float32
 BF16 = jnp.bfloat16
 MESH = pl.DeviceIdType.MESH
@@ -77,18 +77,17 @@
             src_ref=src, dst_ref=dst, send_sem=send, recv_sem=recv, device_id=device, device_id_type=MESH
         )
 
-    def fetch(q):
-        part = pl.ds(q * zq, zq)
-        return (
-            pltpu.make_async_copy(heat_hbm.at[part], heat.at[part], heat_sem.at[q]),
-            pltpu.make_async_copy(density_hbm.at[part], density.at[part], density_sem.at[q]),
-        )
-
+    head_part, tail_part = pl.ds(0, zq), pl.ds(zq, slices - zq)
+    heat_loads = [
+        pltpu.make_async_copy(heat_hbm.at[part], heat.at[part], heat_sem.at[i])
+        for i, part in enumerate((head_part, tail_part))
+    ]
+    density_load = pltpu.make_async_copy(density_hbm, density, density_sem)
     scalars = [(order_hbm, order), (count_hbm, count), (emit_hbm, emit), (albedo_hbm, albedo)]
     loads = [pltpu.make_async_copy(src, dst, scalar_sem.at[i]) for i, (src, dst) in enumerate(scalars)]
+    heat_loads[0].start()
     loads[0].start()
     loads[1].start()
-    fetch(0)[0].start()
 
     barrier = pltpu.get_barrier_semaphore()
 
@@ -96,12 +95,7 @@
     for device in greeted:
         pl.semaphore_signal(barrier, inc=1, device_id=device, device_id_type=MESH)
 
-    for q in range(1, QUARTERS):
-        fetch(q)[0].start()
-    for q in range(QUARTERS):
-        fetch(q)[1].start()
-    loads[2].start()
-    loads[3].start()
+    heat_loads[1].start()
 
     rounds = [x_beside] * (columns // 2 - 1) + [z_beside] * (planes // 2)
 
@@ -136,7 +130,8 @@
     blocks[tile, 0:HEAD, :] = info.astype(F32).astype(BF16)
 
     def pack(q):
-        fetch(q)[0].wait()
+        if q < 2:
+            heat_loads[q].wait()
         pieces = [
             heat[q * zq : (q + 1) * zq, m * BW : (m + 1) * BW, :].reshape(rows, breadth) for m in range(across)
         ]
@@ -208,6 +203,9 @@
                     send(n, sign).start()
         own_part(q, tile).start()
     pass_word(0)
+    density_load.start()
+    loads[2].start()
+    loads[3].start()
 
     offset = iota((BW, breadth), 0) - iota((BW, breadth), 1)
     turn = (offset * offset) % (2 * BW)
@@ -217,8 +215,7 @@
     ratio_y = (row - lane).astype(F32) / (height / 4.0)
     table_y[...] = (cosines[...] / (1.0 + ratio_y * ratio_y)).astype(BF16)
 
-    for q in range(QUARTERS):
-        fetch(q)[1].wait()
+    density_load.wait()
     unit = 1.5 / (slices * depth_count)
     strip = 32
 
@@ -347,9 +344,11 @@
     running = finish(3, finish(1, running))
     for d in range(depth_count):
         late_out[d] = running[d * band : (d + 1) * band, :]
-
-    for a, b in far_first:
-        leaving(late_part, a, b).start()
+    for d in range(depth_count):
+
+        @pl.when(depth != d)
+        def _():
+            late_part(d, depth).start()
 
     late_in[depth] = late_out[depth]
 
@@ -400,7 +399,7 @@
             pltpu.VMEM((depth_count, band, breadth), F32),
             pltpu.VMEM((depth_count, band, breadth), F32),
             pltpu.VMEM((3, band, breadth), F32),
-            dma((4,)), dma((QUARTERS,)), dma((QUARTERS,)),
+            dma((4,)), dma((2,)), dma,
             dma((QUARTERS,)), dma((QUARTERS,)),
             dma((steps,)), dma((steps,)), dma((steps,)), dma((steps,)),
             dma((steps,)), dma((steps,)), dma((steps,)), dma((steps,)),

time: 44.7 us -> 44.5 us (level)
  no operation moved by 1% of the time
where the time goes in v5:
time: 44.5 us; the launch traced here: 44.3 us
  Pallas kernels  43 us (97%)
  between operations  0.73 us (2%)
  local copies, waits for them, and re-layouts  0.61 us (1%)
    pallas_call x1, Pallas kernels, shards(): pl.pallas_call(functools.partial(render, depth_count, tile_count), out_sh...  43 us

profile of v5, /device:TPU:1, one launch (start us, length us, event | category | flops | bytes accessed | tf_op | source)
XLA Modules:
  0.0 44.3 jit_solution(14936002179707690374)
XLA Ops:
  0.0 0.0 copy-start.2
  0.0 0.0 copy-start.1
  0.0 0.0 copy-start
  0.7 0.0 copy-done.2
  0.7 0.0 copy-done.1
  0.7 0.0 copy-done
  0.7 43.0 %shard_map.64 = f32[4,4,128]{2,1,0:T(4,128)S(1)} custom-call(bf16[32,128,128]{2,1,0:T(8,128)(2,1)} %density_hbm.1, bf16[32,128,128]{2,1,0:T(8,128)(2,1)} %heat_hbm.1, f32[3]{0:T(128)S(1)} %copy-done, f32[3]{0:T(128)S(1)} %copy-done.1, s32[1,16]{1,0:T(1,128)S(1)} %copy-done.2, s32[1]{0:T(128)S(6)} %copy.9.count_hbm), custom_call_target="tpu_custom_call" | custom-call | flops 3000000000 | bytes 2097152 | tf_op jit(solution)/shard_map/pallas_call | solution.py:380
  43.7 0.6 %copy.10 = f32[4,1,512]{2,1,0:T(1,128)} copy(f32[4,1,512]{2,1,0:T(1,128)S(1)} %bitcast.1) | data formatting | bytes 16384
Async XLA Ops:
  0.0 0.7 %copy-start.2 = (s32[1,16]{1,0:T(1,128)S(1)}, s32[1,16]{1,0:T(1,128)}, u32[]{:S(2)}) copy-start(s32[1,16]{1,0:T(1,128)} %order_hbm.1) | copy-start | bytes 196
  0.0 0.7 %copy-start.1 = (f32[3]{0:T(128)S(1)}, f32[3]{0:T(128)}, u32[]{:S(2)}) copy-start(f32[3]{0:T(128)} %albedo_hbm.1) | copy-start | bytes 40
  0.0 0.7 %copy-start = (f32[3]{0:T(128)S(1)}, f32[3]{0:T(128)}, u32[]{:S(2)}) copy-start(f32[3]{0:T(128)} %emit_hbm.1) | copy-start | bytes 40

commit v6 on v5

--- a/solution.py
+++ b/solution.py
@@ -283,14 +283,17 @@
                 build(source)
             spread[quarter] += product(source, quarter)
 
-    def finish(q, running):
-        mats = []
-        for z in range(zq):
-            flat = spread[q, z * BW : (z + 1) * BW, :].astype(BF16)
-            mats.append(jnp.concatenate([flat[:, m * breadth : (m + 1) * breadth] for m in range(across)], axis=0))
+    def finish(quarters, running):
+        mats, slabs = [], []
+        for q in quarters:
+            for z in range(zq):
+                flat = spread[q, z * BW : (z + 1) * BW, :].astype(BF16)
+                pieces = [flat[:, m * breadth : (m + 1) * breadth] for m in range(across)]
+                mats.append(jnp.concatenate(pieces, axis=0))
+                slabs.append(q * zq + z)
         inscatter = jnp.dot(table_y[...], jnp.concatenate(mats, axis=1), preferred_element_type=F32)
-        for z in range(zq):
-            running = running + weight[q * zq + z] * inscatter[:, z * breadth : (z + 1) * breadth]
+        for i, z in enumerate(slabs):
+            running = running + weight[z] * inscatter[:, i * breadth : (i + 1) * breadth]
         return running
 
     def gather_early():
@@ -339,9 +342,9 @@
 
     for n in range(steps - BEHIND, steps - 1):
         collect(n)
-    running = finish(2, finish(0, jnp.zeros((height, breadth), F32)))
+    running = finish((0, 2), jnp.zeros((height, breadth), F32))
     collect(steps - 1)
-    running = finish(3, finish(1, running))
+    running = finish((1, 3), running)
     for d in range(depth_count):
         late_out[d] = running[d * band : (d + 1) * band, :]
     for d in range(depth_count):

time: 44.5 us -> 44.5 us (level)
  no operation moved by 1% of the time
where the time goes in v6:
time: 44.5 us; the launch traced here: 44.3 us
  Pallas kernels  43 us (97%)
  between operations  0.73 us (2%)
  local copies, waits for them, and re-layouts  0.61 us (1%)
    pallas_call x1, Pallas kernels, shards(): pl.pallas_call(functools.partial(render, depth_count, tile_count), out_sh...  43 us

profile of v6, /device:TPU:1, one launch (start us, length us, event | category | flops | bytes accessed | tf_op | source)
XLA Modules:
  0.0 44.3 jit_solution(14936002179707690374)
XLA Ops:
  0.0 0.0 copy-start.2
  0.0 0.0 copy-start.1
  0.0 0.0 copy-start
  0.7 0.0 copy-done.2
  0.7 0.0 copy-done.1
  0.7 0.0 copy-done
  0.7 43.0 %shard_map.64 = f32[4,4,128]{2,1,0:T(4,128)S(1)} custom-call(bf16[32,128,128]{2,1,0:T(8,128)(2,1)} %density_hbm.1, bf16[32,128,128]{2,1,0:T(8,128)(2,1)} %heat_hbm.1, f32[3]{0:T(128)S(1)} %copy-done, f32[3]{0:T(128)S(1)} %copy-done.1, s32[1,16]{1,0:T(1,128)S(1)} %copy-done.2, s32[1]{0:T(128)S(6)} %copy.9.count_hbm), custom_call_target="tpu_custom_call" | custom-call | flops 3000000000 | bytes 2097152 | tf_op jit(solution)/shard_map/pallas_call | solution.py:383
  43.7 0.6 %copy.10 = f32[4,1,512]{2,1,0:T(1,128)} copy(f32[4,1,512]{2,1,0:T(1,128)S(1)} %bitcast.1) | data formatting | bytes 16384
Async XLA Ops:
  0.0 0.7 %copy-start.2 = (s32[1,16]{1,0:T(1,128)S(1)}, s32[1,16]{1,0:T(1,128)}, u32[]{:S(2)}) copy-start(s32[1,16]{1,0:T(1,128)} %order_hbm.1) | copy-start | bytes 196
  0.0 0.7 %copy-start.1 = (f32[3]{0:T(128)S(1)}, f32[3]{0:T(128)}, u32[]{:S(2)}) copy-start(f32[3]{0:T(128)} %albedo_hbm.1) | copy-start | bytes 40
  0.0 0.7 %copy-start = (f32[3]{0:T(128)S(1)}, f32[3]{0:T(128)}, u32[]{:S(2)}) copy-start(f32[3]{0:T(128)} %emit_hbm.1) | copy-start | bytes 40
